TPU v7x, 256 devices: a whole 4x4x8 slice. The times are simulated.
256 devices in a mesh: shard: 64 (over y, z, core), sub: 4 (over x).
Axes of the slice: x: 4, y: 4, z: 8, core: 2. Of those that a mesh axis runs over, the one named last changes fastest.
Arguments:
- points: bfloat16 [262144, 768], P(('shard', 'sub'))
- centroids: float32 [262144, 768], P(('shard', 'sub')), may hold values from -6 to 6
- cand_peer: int32 [1024, 4], P(('shard', 'sub')), may hold values from 0 to 63, as said below
- cand_block: int32 [1024, 4], P(('shard', 'sub')), may hold values from 0 to 7
Outputs:
- refined: float32 [262144, 768], P(('shard', 'sub'))
Inputs may be any that keep to these rules, and one draw needn't show every extreme that they name: The owner of a candidate is the device with shard index cand_peer and the sub index of the requesting device. The 4 peers of one point block differ. All requests of one device to one peer name the same block.
All inputs are finite; a program needn't handle non-finite values.
Results may differ from a plain program's by a relative error of at most 0.0011.
Values may be sent and summed in bfloat16 or wider, within the bound.
A program may use at most 128 MiB of HBM per device.

v0:
```python
import jax
import jax.numpy as jnp
from jax import lax
from jax.sharding import PartitionSpec as P

PBLK = 256
CBLK = 128
CAND = 4


def on_device(points, centroids, cand_peer, cand_block):
    peers_count = lax.axis_size("shard")
    total_points = points.shape[0] * peers_count * lax.axis_size("sub")
    blocks_here = points.shape[0] // PBLK
    owned_blocks = centroids.shape[0] // CBLK
    width = points.shape[1]
    peer_ids = jnp.arange(peers_count, dtype=jnp.int32)
    owned_ids = jnp.arange(owned_blocks, dtype=jnp.int32)
    hits = cand_peer[:, :, None] == peer_ids[None, None, :]
    wanted = jnp.max(jnp.where(hits, cand_block[:, :, None], -1), axis=(0, 1))
    asked = lax.all_to_all(wanted, "shard", split_axis=0, concat_axis=0, tiled=True)
    half = centroids.astype(jnp.bfloat16).reshape(owned_blocks, CBLK * width)
    pick_table = (asked[:, None] == owned_ids[None, :]).astype(jnp.bfloat16)
    outgoing = jnp.dot(pick_table, half, preferred_element_type=jnp.bfloat16).reshape(
        peers_count, CBLK, width
    )
    fetched = lax.all_to_all(outgoing, "shard", split_axis=0, concat_axis=0, tiled=True)
    chosen = jnp.take(fetched, cand_peer, axis=0).reshape(blocks_here, CAND * CBLK, width)
    rows = points.reshape(blocks_here, PBLK, width)
    row_sq = jnp.sum(jnp.square(rows.astype(jnp.float32)), axis=-1)
    col_sq = jnp.sum(jnp.square(chosen.astype(jnp.float32)), axis=-1)
    dots = jnp.einsum("bpd,bcd->bpc", rows, chosen, preferred_element_type=jnp.float32)
    dist = row_sq[:, :, None] + col_sq[:, None, :] - 2.0 * dots
    gap_total = jnp.sum(jnp.mean(dist, axis=2) - jnp.min(dist, axis=2))
    spread = lax.psum(gap_total, ("shard", "sub")) / total_points + 1e-06
    logits = -3.0 * (dist - jnp.min(dist, axis=2, keepdims=True)) / spread
    resp = jax.nn.softmax(logits, axis=2).astype(jnp.bfloat16)
    part = jnp.einsum("bpc,bpd->bcd", resp, rows, preferred_element_type=jnp.float32)
    mass = jnp.sum(resp.astype(jnp.float32), axis=1)
    part = part.reshape(blocks_here * CAND, CBLK * width)
    mass = mass.reshape(blocks_here * CAND, CBLK)
    slot_index = cand_peer.reshape(-1)
    slot_table = (peer_ids[:, None] == slot_index[None, :]).astype(jnp.float32)
    slot_sums = jnp.dot(
        slot_table, part, preferred_element_type=jnp.float32, precision=lax.Precision.HIGHEST
    )
    slot_mass = jnp.dot(
        slot_table, mass, preferred_element_type=jnp.float32, precision=lax.Precision.HIGHEST
    )
    slot_sums = slot_sums.astype(jnp.bfloat16).reshape(peers_count, CBLK, width)
    slot_mass = slot_mass.astype(jnp.bfloat16)
    back_sums, back_mass = (
        lax.all_to_all(slot_sums, "shard", split_axis=0, concat_axis=0, tiled=True),
        lax.all_to_all(slot_mass, "shard", split_axis=0, concat_axis=0, tiled=True),
    )
    home_table = (owned_ids[:, None] == asked[None, :]).astype(jnp.bfloat16)
    own_sums = jnp.dot(
        home_table, back_sums.reshape(peers_count, CBLK * width), preferred_element_type=jnp.float32
    )
    own_mass = jnp.dot(home_table, back_mass, preferred_element_type=jnp.float32)
    own_sums = own_sums.reshape(owned_blocks * CBLK, width)
    own_mass = own_mass.reshape(owned_blocks * CBLK)
    return (own_sums + 1.0 * centroids) / (own_mass + 1.0)[:, None]


def solution(mesh):
    placed = (
        P(("shard", "sub"), None),
        P(("shard", "sub"), None),
        P(("shard", "sub"), None),
        P(("shard", "sub"), None),
    )
    return jax.shard_map(
        on_device, mesh=mesh, in_specs=placed, out_specs=P(("shard", "sub"), None), check_vma=False
    )
```

profile of v0, /device:TPU:1, one launch (start us, length us, event | category | flops | bytes accessed | tf_op | source)
XLA Modules:
  0.0 769.0 jit_solution(8501271960190376971)
XLA Ops:
  1.5 13.2 %all-to-all-start = ((s32[64,1,1]{2,1,0:T(1,128)}), s32[64,1,1]{2,1,0:T(1,128)S(1)}, u32[]{:S(2)}, u32[]{:S(2)}) async-start(s32[64,1,1]{2,1,0:T(1,128)} %copy.12), calls=%async_computation | async-start | bytes 65536 | tf_op jit(solution)/shard_map/all_to_all | solution.py:21
  14.7 2.0 convert_element_type.27
  17.4 6.4 all-to-all-done
  23.9 1.2 reduce.2
  25.1 3.7 fusion.10
  28.8 22.8 %copy.13 = bf16[64,128,768]{2,1,0:T(8,128)(2,1)} copy(bf16[64,128,768]{2,0,1:T(8,128)(2,1)S(1)} %fusion.10) | data formatting | bytes 25165824 | tf_op jit(solution)/shard_map/dot_general | solution.py:24
  51.7 6.0 all-to-all-start.1
  58.2 275.1 %all-to-all-done.1 = bf16[64,128,768]{2,1,0:T(8,128)(2,1)} async-done(((bf16[64,128,768]{2,1,0:T(8,128)(2,1)}), bf16[64,128,768]{2,1,0:T(8,128)(2,1)}, u32[]{:S(2)}, u32[]{:S(2)}) %all-to-all-start.1) | async-done | bytes 12582944 | tf_op jit(solution)/shard_map/all_to_all | solution.py:27
  333.3 5.3 gather_fusion
  341.0 1.1 fusion.16
  342.8 75.8 %psum.7 = f32[]{:T(128)} all-reduce(f32[]{:T(128)} %subtract_reduce_fusion), channel_id=1, replica_groups=mesh['shard'=64,'sub'=4] {'shard','sub'}, use_global_device_ids=true, to_apply=%region_6.7 | all-reduce | flops 1 | bytes 8 | tf_op jit(solution)/shard_map/psum | solution.py:35
  419.3 1.3 fusion.17
  421.0 1.0 copy-done.3
  422.0 3.6 fusion.18
  425.7 5.1 reshape.63
  431.6 5.5 all-to-all-start.3
  437.1 15.5 %convolution_convert_fusion = bf16[64,98304]{1,0:T(8,128)(2,1)S(1)} fusion(f32[16,98304]{1,0:T(8,128)} %reshape.63, s32[16]{0:T(128)S(1)} %eq.64), kind=kOutput, calls=%fused_computation.2 | convolution fusion | flops 1214252032 | bytes 18874432 | tf_op jit(solution)/shard_map/dot_general | solution.py:44
  452.6 6.5 copy.18
  459.1 10.5 %all-to-all-start.2 = ((bf16[64,128,768]{2,1,0:T(8,128)(2,1)}), bf16[64,128,768]{2,1,0:T(8,128)(2,1)}, u32[]{:S(2)}, u32[]{:S(2)}) async-start(bf16[64,128,768]{2,1,0:T(8,128)(2,1)} %bitcast.42), calls=%async_computation.2 | async-start | bytes 25165824 | tf_op jit(solution)/shard_map/all_to_all | solution.py:53
  469.7 275.5 %all-to-all-done.2 = bf16[64,128,768]{2,1,0:T(8,128)(2,1)} async-done(((bf16[64,128,768]{2,1,0:T(8,128)(2,1)}), bf16[64,128,768]{2,1,0:T(8,128)(2,1)}, u32[]{:S(2)}, u32[]{:S(2)}) %all-to-all-start.2) | async-done | bytes 12582944 | tf_op jit(solution)/shard_map/all_to_all | solution.py:53
  745.3 12.2 %copy.19 = bf16[8,8,128,768]{3,1,2,0:T(8,128)(2,1)S(1)} copy(bf16[8,8,128,768]{3,2,1,0:T(8,128)(2,1)} %bitcast.18) | data formatting | bytes 25165824
  757.5 3.4 fusion.8
  760.9 4.2 reshape.66
  765.0 3.9 add_divide_fusion
  (31 shorter events, 7.1 us)
Async XLA Ops:
  1.5 22.4 %all-to-all-start = ((s32[64,1,1]{2,1,0:T(1,128)}), s32[64,1,1]{2,1,0:T(1,128)S(1)}, u32[]{:S(2)}, u32[]{:S(2)}) async-start(s32[64,1,1]{2,1,0:T(1,128)} %copy.12), calls=%async_computation | async-start | bytes 65536 | tf_op jit(solution)/shard_map/all_to_all | solution.py:21
  51.7 6.0 copy-start.4
  51.7 6.2 copy-start.1
  51.7 281.7 %all-to-all-start.1 = ((bf16[64,128,768]{2,1,0:T(8,128)(2,1)}), bf16[64,128,768]{2,1,0:T(8,128)(2,1)}, u32[]{:S(2)}, u32[]{:S(2)}) async-start(bf16[64,128,768]{2,1,0:T(8,128)(2,1)} %copy.13), calls=%async_computation.1 | async-start | bytes 25165824 | tf_op jit(solution)/shard_map/all_to_all | solution.py:27
  339.6 1.4 copy-start.2
  420.6 1.4 copy-start.3
  431.6 27.5 %all-to-all-start.3 = ((bf16[64,1,128]{2,1,0:T(2,128)(2,1)}), bf16[64,1,128]{2,1,0:T(2,128)(2,1)S(1)}, u32[]{:S(2)}, u32[]{:S(2)}) async-start(bf16[64,1,128]{2,1,0:T(2,128)(2,1)} %copy.14), calls=%async_computation.3 | async-start | bytes 65536 | tf_op jit(solution)/shard_map/all_to_all | solution.py:54
  459.1 286.2 %all-to-all-start.2 = ((bf16[64,128,768]{2,1,0:T(8,128)(2,1)}), bf16[64,128,768]{2,1,0:T(8,128)(2,1)}, u32[]{:S(2)}, u32[]{:S(2)}) async-start(bf16[64,128,768]{2,1,0:T(8,128)(2,1)} %bitcast.42), calls=%async_computation.2 | async-start | bytes 25165824 | tf_op jit(solution)/shard_map/all_to_all | solution.py:53
  760.9 4.2 copy-start
where the time goes:
time: 770 us; the launch traced here: 769 us
  waiting for transfers between devices  557 us (72%)
  blocking collectives  75.8 us (10%)
  local copies, waits for them, and re-layouts  60.5 us (8%)
  starting transfers between devices  35.1 us (5%)
  matrix products  27.6 us (4%)
  other arithmetic  12.2 us (2%)
    all_to_all x1, waiting for transfers between devices, on_device(): lax.all_to_all(slot_sums, 'shard', split_axis=0, concat_axis=0, tiled=True)  276 us
    all_to_all x1, waiting for transfers between devices, on_device(): lax.all_to_all(outgoing, 'shard', split_axis=0, concat_axis=0, tiled=True)  275 us
    psum x1, blocking collectives, on_device(): spread = lax.psum(gap_total, ('shard', 'sub')) / total_points + 1e-06  75.8 us
    dot_general x1, local copies, waits for them, and re-layouts, on_device(): jnp.dot(pick_table, half, preferred_element_type=jnp.bfloat16)  22.8 us
    unnamed x15, local copies, waits for them, and re-layouts  20.8 us
    dot_general x1, matrix products, on_device(): jnp.dot(slot_table, part, preferred_element_type=jnp.float32, precision=l...  15.5 us
  transfers between devices with their start and end apart: 4, of which 3 were waited for; matrix products, arithmetic and copies ran while one was open for 3% of the time, Pallas kernels for 0%

commit v1 on v0

v1 whole, which is shorter than its diff:
```python
import functools

import jax
import jax.numpy as jnp
from jax import lax
from jax.experimental import pallas as pl
from jax.experimental.pallas import tpu as pltpu
from jax.sharding import PartitionSpec as P

PBLK = 256
CBLK = 128
CAND = 4
NY, NZ, NC = 4, 8, 2
NQ = 3
LANES = 128
OWNED = 8
SLOTS = 16
VMEM_LIMIT = 60 * 1024 * 1024
MESH = pl.DeviceIdType.MESH


def wait_bytes(ref, sem):
    pltpu.make_async_copy(ref, ref, sem).wait()


def kernel(
    ny,
    nz,
    nx,
    total_points,
    x_ref,
    h_ref,
    xsq_ref,
    req_ref,
    mask_ref,
    out_ref,
    outw_ref,
    rq,
    onehot,
    onehot_t,
    held,
    pick,
    got,
    dist,
    csq,
    resp,
    back,
    part,
    final,
    home,
    w_pick,
    w_back,
    w_sum,
    w_part,
    w_final,
    w_home,
    gap_own,
    gap_row,
    gap_y,
    gap_x,
    send_sem,
    recv_sem,
):
    nk = nz * NC
    rp = CBLK // nz // 2
    pts = x_ref.shape[0]
    keys = ny * nk * SLOTS
    f32 = jnp.float32
    bf16 = jnp.bfloat16
    shard = lax.axis_index("shard")
    sub = lax.axis_index("sub")
    my_y = lax.div(shard, nk)
    my_k = lax.rem(shard, nk)

    def row_dev(k):
        return (my_y * nk + k, sub)

    def y_dev(y):
        return (y * nk + my_k, sub)

    barrier = pltpu.get_barrier_semaphore()

    def greet_row(off, carry):
        pl.semaphore_signal(
            barrier, inc=1, device_id=row_dev(lax.rem(my_k + off, nk)), device_id_type=MESH
        )
        return carry

    lax.fori_loop(1, nk, greet_row, 0)
    for off in range(1, ny):
        pl.semaphore_signal(
            barrier, inc=1, device_id=y_dev(lax.rem(my_y + off, ny)), device_id_type=MESH
        )
    for off in range(1, nx):
        pl.semaphore_signal(
            barrier, inc=1, device_id=(shard, lax.rem(sub + off, nx)), device_id_type=MESH
        )
    pl.semaphore_wait(barrier, nk - 1 + ny - 1 + nx - 1)

    def row_send(src_of, dst_of, sem):
        def body(off, carry):
            k = lax.rem(my_k + off, nk)
            pltpu.make_async_remote_copy(
                src_ref=src_of(k),
                dst_ref=dst_of(my_k),
                send_sem=send_sem.at[sem],
                recv_sem=recv_sem.at[sem],
                device_id=row_dev(k),
                device_id_type=MESH,
            ).start()
            return carry

        lax.fori_loop(1, nk, body, 0)
        pltpu.make_async_copy(src_of(my_k), dst_of(my_k), recv_sem.at[sem]).start()

    def y_send(src_of, dst_ref, sem):
        for off in range(1, ny):
            y = lax.rem(my_y + off, ny)
            pltpu.make_async_remote_copy(
                src_ref=src_of(y),
                dst_ref=dst_ref,
                send_sem=send_sem.at[sem],
                recv_sem=recv_sem.at[sem],
                device_id=y_dev(y),
                device_id_type=MESH,
            ).start()

    REQ, GAP_ROW, GAP_Y, GAP_X, W4, W5, W6 = 0, 1, 2, 3, 4, 5, 6
    S1, S2, S3, S4, S5, S6 = (7 + NQ * s for s in range(6))

    row_send(lambda k: req_ref, lambda k: rq.at[k], REQ)
    for q in range(NQ):
        row_send(lambda k: h_ref.at[q, k], lambda k: held.at[q, my_y, k], S1 + q)

    wait_bytes(rq, recv_sem.at[REQ])

    def build(d, carry):
        code = rq[d]
        lane = lax.broadcasted_iota(jnp.int32, (SLOTS, LANES), 1)
        for t in range(keys // LANES):
            for par in range(2):
                hit = code + OWNED * par == lane + t * LANES
                onehot[d, par * SLOTS : (par + 1) * SLOTS, t * LANES : (t + 1) * LANES] = (
                    jnp.where(hit, 1.0, 0.0).astype(bf16)
                )
        return carry

    lax.fori_loop(0, nk, build, 0)
    for t in range(nk * 2 * SLOTS // LANES):
        block = onehot[4 * t : 4 * t + 4].reshape(LANES, keys).astype(f32)
        onehot_t[:, t * LANES : (t + 1) * LANES] = block.T.astype(bf16)

    for q in range(NQ):
        wait_bytes(held.at[q, my_y], recv_sem.at[S1 + q])
        y_send(lambda y: held.at[q, my_y], held.at[q, my_y], S2 + q)

    for q in range(NQ):
        wait_bytes(held.at[q, pl.ds(0, ny - 1)], recv_sem.at[S2 + q])

        def select(p, carry):
            left = held[q, :, :, 2 * p].reshape(keys, LANES)
            right = held[q, :, :, 2 * p + 1].reshape(keys, LANES)
            both = jnp.concatenate([left, right], axis=1)
            table = onehot[...].reshape(nk * 2 * SLOTS, keys)
            chosen = jnp.dot(table, both, preferred_element_type=f32).astype(bf16)
            pick[q, :, 2 * p] = chosen[:, :LANES].reshape(nk, 2 * SLOTS, LANES)
            pick[q, :, 2 * p + 1] = chosen[:, LANES:].reshape(nk, 2 * SLOTS, LANES)
            return carry

        lax.fori_loop(0, rp // 2, select, 0)
        row_send(lambda k: pick.at[q, k], lambda k: got.at[q, k], S3 + q)

    rows = rp * 2 * SLOTS
    for q in range(NQ):
        wait_bytes(got.at[q], recv_sem.at[S3 + q])

        def multiply(g, carry):
            left = got[q, 2 * g].reshape(rows, LANES)
            right = got[q, 2 * g + 1].reshape(rows, LANES)
            both = jnp.concatenate([left, right], axis=1)
            dots = lax.dot_general(
                both,
                x_ref[:, q * 2 * LANES : (q + 1) * 2 * LANES],
                (((1,), (1,)), ((), ())),
                preferred_element_type=f32,
            ).reshape(2 * rp, SLOTS, pts)
            square = jnp.square(left.astype(f32)) + jnp.square(right.astype(f32))
            square = square.reshape(2 * rp, SLOTS, LANES)
            here = pl.ds(g * 2 * rp, 2 * rp)
            if q == 0:
                dist[here] = dots
                csq[here] = square
            else:
                dist[here] = dist[here] + dots
                csq[here] = csq[here] + square
            return carry

        lax.fori_loop(0, nz, multiply, 0)

    groups = nz * 2 * rp

    def measure(i, carry):
        least, total = carry
        valid = mask_ref[...] > 0.5
        col = jnp.sum(csq[i], axis=1, keepdims=True)
        d = (xsq_ref[...] + col) - 2.0 * dist[i]
        far = jnp.where(valid, d, jnp.inf)
        dist[i] = far
        return jnp.minimum(least, far), total + jnp.where(valid, d, 0.0)

    least, total = lax.fori_loop(
        0,
        groups,
        measure,
        (jnp.full((SLOTS, pts), jnp.inf, f32), jnp.zeros((SLOTS, pts), f32)),
    )
    least = jnp.min(least, axis=0, keepdims=True)
    total = jnp.sum(total, axis=0, keepdims=True)
    gap = jnp.sum(total / (CAND * CBLK) - least, axis=1, keepdims=True)

    gap_own[0] = jnp.broadcast_to(gap, (8, LANES))
    row_send(lambda k: gap_own.at[0], lambda k: gap_row.at[k], GAP_ROW)
    wait_bytes(gap_row, recv_sem.at[GAP_ROW])
    gap_own[1] = jnp.sum(gap_row[...], axis=0)
    gap_y[my_y] = gap_own[1]
    y_send(lambda y: gap_own.at[1], gap_y.at[my_y], GAP_Y)
    wait_bytes(gap_y.at[pl.ds(0, ny - 1)], recv_sem.at[GAP_Y])
    gap_own[2] = jnp.sum(gap_y[...], axis=0)
    gap_x[sub] = gap_own[2]
    for off in range(1, nx):
        pltpu.make_async_remote_copy(
            src_ref=gap_own.at[2],
            dst_ref=gap_x.at[sub],
            send_sem=send_sem.at[GAP_X],
            recv_sem=recv_sem.at[GAP_X],
            device_id=(shard, lax.rem(sub + off, nx)),
            device_id_type=MESH,
        ).start()
    if nx > 1:
        wait_bytes(gap_x.at[pl.ds(0, nx - 1)], recv_sem.at[GAP_X])
    spread = jnp.sum(gap_x[...], axis=0)[:1, :1] / total_points + 1e-6
    scale = 3.0 / spread

    def exponent(i, norm):
        e = jnp.exp((least - dist[i]) * scale)
        dist[i] = e
        return norm + e

    norm = lax.fori_loop(0, groups, exponent, jnp.zeros((SLOTS, pts), f32))
    inverse = 1.0 / jnp.sum(norm, axis=0, keepdims=True)

    def normalise(i, carry):
        resp[i] = (dist[i] * inverse).astype(bf16)
        return carry

    lax.fori_loop(0, groups, normalise, 0)

    for q in range(NQ):
        wait_bytes(pick.at[q, pl.ds(0, nk - 1)], send_sem.at[S3 + q])

        def accumulate(g, carry):
            here = resp[pl.ds(g * 2 * rp, 2 * rp)].reshape(rows, pts)
            sums = jnp.dot(
                here, x_ref[:, q * 2 * LANES : (q + 1) * 2 * LANES], preferred_element_type=f32
            ).astype(bf16)
            pick[q, 2 * g] = sums[:, :LANES].reshape(rp, 2 * SLOTS, LANES)
            pick[q, 2 * g + 1] = sums[:, LANES:].reshape(rp, 2 * SLOTS, LANES)
            if q == 0:
                mass = jnp.dot(here, jnp.ones((pts, LANES), bf16), preferred_element_type=f32)
                mass = mass.reshape(rp, 2 * SLOTS, LANES)
                lane = lax.broadcasted_iota(jnp.int32, (2 * SLOTS, LANES), 1)
                packed = jnp.zeros((2 * SLOTS, LANES), f32)
                for r in range(rp):
                    packed = jnp.where(lane == r, mass[r], packed)
                w_pick[g] = packed.astype(bf16)
            return carry

        lax.fori_loop(0, nz, accumulate, 0)
        row_send(lambda k: pick.at[q, k], lambda k: back.at[q, k], S4 + q)
    row_send(lambda k: w_pick.at[lax.div(k, NC)], lambda k: w_back.at[k], W4)

    for q in range(NQ):
        wait_bytes(held.at[q, pl.ds(0, ny - 1)], send_sem.at[S2 + q])
        wait_bytes(back.at[q], recv_sem.at[S4 + q])

        def combine(p, carry):
            left = back[q, :, 2 * p].reshape(nk * 2 * SLOTS, LANES)
            right = back[q, :, 2 * p + 1].reshape(nk * 2 * SLOTS, LANES)
            both = jnp.concatenate([left, right], axis=1)
            added = jnp.dot(onehot_t[...], both, preferred_element_type=f32).astype(bf16)
            held[q, :, :, 2 * p] = added[:, :LANES].reshape(ny, nk, SLOTS, LANES)
            held[q, :, :, 2 * p + 1] = added[:, LANES:].reshape(ny, nk, SLOTS, LANES)
            return carry

        lax.fori_loop(0, rp // 2, combine, 0)
        y_send(lambda y: held.at[q, y], part.at[q, my_y], S5 + q)
    wait_bytes(w_back, recv_sem.at[W4])
    w_sum[...] = jnp.dot(
        onehot_t[...], w_back[...].reshape(nk * 2 * SLOTS, LANES), preferred_element_type=f32
    ).reshape(ny, nk, SLOTS, LANES)
    y_send(lambda y: w_sum.at[y], w_part.at[my_y], W5)

    for q in range(NQ):
        wait_bytes(part.at[q, pl.ds(0, ny - 1)], recv_sem.at[S5 + q])

        def gather(k, carry):
            added = held[q, my_y, k].astype(f32)
            for off in range(1, ny):
                added = added + part[q, lax.rem(my_y + off, ny), k].astype(f32)
            final[q, k] = added.astype(bf16)
            return carry

        lax.fori_loop(0, nk, gather, 0)
        row_send(lambda k: final.at[q, k], lambda k: home.at[q, k], S6 + q)
    wait_bytes(w_part.at[pl.ds(0, ny - 1)], recv_sem.at[W5])
    weight = w_sum[my_y]
    for off in range(1, ny):
        weight = weight + w_part[lax.rem(my_y + off, ny)]
    w_final[...] = weight
    row_send(lambda k: w_final.at[k], lambda k: w_home.at[k], W6)

    for q in range(NQ):
        wait_bytes(home.at[q], recv_sem.at[S6 + q])
        out_ref[q] = home[q]
    wait_bytes(w_home, recv_sem.at[W6])
    outw_ref[...] = w_home[...]

    wait_bytes(rq.at[pl.ds(0, nk - 1)], send_sem.at[REQ])
    wait_bytes(gap_row.at[pl.ds(0, nk - 1)], send_sem.at[GAP_ROW])
    wait_bytes(gap_y.at[pl.ds(0, ny - 1)], send_sem.at[GAP_Y])
    if nx > 1:
        wait_bytes(gap_x.at[pl.ds(0, nx - 1)], send_sem.at[GAP_X])
    wait_bytes(w_back.at[pl.ds(0, nk - 1)], send_sem.at[W4])
    wait_bytes(w_sum.at[pl.ds(0, ny - 1)], send_sem.at[W5])
    wait_bytes(w_final.at[pl.ds(0, nk - 1)], send_sem.at[W6])
    for q in range(NQ):
        wait_bytes(h_ref.at[q, pl.ds(0, nk - 1)], send_sem.at[S1 + q])
        wait_bytes(pick.at[q, pl.ds(0, nk - 1)], send_sem.at[S4 + q])
        wait_bytes(held.at[q, pl.ds(0, ny - 1)], send_sem.at[S5 + q])
        wait_bytes(final.at[q, pl.ds(0, nk - 1)], send_sem.at[S6 + q])


def on_device(ny, nz, nx, points, centroids, cand_peer, cand_block):
    f32, bf16 = jnp.float32, jnp.bfloat16
    nk = nz * NC
    rp = CBLK // nz // 2
    pts, width = points.shape
    blocks_here = pts // PBLK
    total_points = pts * ny * nk * nx
    keys = ny * nk * SLOTS

    peer = cand_peer.reshape(-1)
    same = peer[:, None] == peer[None, :]
    before = jnp.arange(SLOTS)[None, :] < jnp.arange(SLOTS)[:, None]
    first = jnp.logical_not(jnp.any(same & before, axis=1))
    code = jnp.where(first, peer * SLOTS + cand_block.reshape(-1), -(2**20)).astype(jnp.int32)
    req = jnp.broadcast_to(code[:, None], (SLOTS, LANES))
    used = jnp.any(same.reshape(SLOTS, blocks_here, CAND), axis=2) & first[:, None]
    mask = jnp.repeat(used.astype(f32), PBLK, axis=1)

    half = centroids.astype(bf16).reshape(OWNED, nz, rp, 2, NQ, NC, LANES)
    half = half.transpose(4, 1, 5, 2, 3, 0, 6).reshape(NQ, nk, rp, SLOTS, LANES)
    xsq = jnp.sum(jnp.square(points.astype(f32)), axis=1)[None, :]

    vmem = pl.BlockSpec(memory_space=pltpu.VMEM)
    n_sem = 7 + 6 * NQ
    sums, weights = pl.pallas_call(
        functools.partial(kernel, ny, nz, nx, total_points),
        out_shape=(
            jax.ShapeDtypeStruct((NQ, nk, rp, SLOTS, LANES), bf16),
            jax.ShapeDtypeStruct((nk, SLOTS, LANES), f32),
        ),
        in_specs=[vmem] * 5,
        out_specs=(vmem, vmem),
        scratch_shapes=[
            pltpu.VMEM((nk, SLOTS, LANES), jnp.int32),
            pltpu.VMEM((nk, 2 * SLOTS, keys), bf16),
            pltpu.VMEM((keys, nk * 2 * SLOTS), bf16),
            pltpu.VMEM((NQ, ny, nk, rp, SLOTS, LANES), bf16),
            pltpu.VMEM((NQ, nk, rp, 2 * SLOTS, LANES), bf16),
            pltpu.VMEM((NQ, nk, rp, 2 * SLOTS, LANES), bf16),
            pltpu.VMEM((nz * 2 * rp, SLOTS, pts), f32),
            pltpu.VMEM((nz * 2 * rp, SLOTS, LANES), f32),
            pltpu.VMEM((nz * 2 * rp, SLOTS, pts), bf16),
            pltpu.VMEM((NQ, nk, rp, 2 * SLOTS, LANES), bf16),
            pltpu.VMEM((NQ, ny, nk, rp, SLOTS, LANES), bf16),
            pltpu.VMEM((NQ, nk, rp, SLOTS, LANES), bf16),
            pltpu.VMEM((NQ, nk, rp, SLOTS, LANES), bf16),
            pltpu.VMEM((nz, 2 * SLOTS, LANES), bf16),
            pltpu.VMEM((nk, 2 * SLOTS, LANES), bf16),
            pltpu.VMEM((ny, nk, SLOTS, LANES), f32),
            pltpu.VMEM((ny, nk, SLOTS, LANES), f32),
            pltpu.VMEM((nk, SLOTS, LANES), f32),
            pltpu.VMEM((nk, SLOTS, LANES), f32),
            pltpu.VMEM((3, 8, LANES), f32),
            pltpu.VMEM((nk, 8, LANES), f32),
            pltpu.VMEM((ny, 8, LANES), f32),
            pltpu.VMEM((nx, 8, LANES), f32),
            pltpu.SemaphoreType.DMA((n_sem,)),
            pltpu.SemaphoreType.DMA((n_sem,)),
        ],
        compiler_params=pltpu.CompilerParams(
            collective_id=0, has_side_effects=True, vmem_limit_bytes=VMEM_LIMIT
        ),
    )(points, half, xsq, req, mask)

    sums = sums.reshape(NQ, nz, NC, rp, 2, OWNED, LANES).transpose(5, 1, 3, 4, 0, 2, 6)
    sums = sums.reshape(OWNED * CBLK, width).astype(f32)
    weights = weights.reshape(nz, NC, 2, OWNED, LANES)[:, 0, :, :, :rp].transpose(2, 0, 3, 1)
    weights = weights.reshape(OWNED * CBLK)
    return (sums + 1.0 * centroids) / (weights + 1.0)[:, None]


def solution(mesh):
    placed = P(("shard", "sub"), None)
    body = functools.partial(on_device, NY, NZ, mesh.shape["sub"])
    return jax.shard_map(
        body, mesh=mesh, in_specs=(placed,) * 4, out_specs=placed, check_vma=False
    )
```

time: 770 us -> 312 us (0.41)
  waiting for transfers between devices: 557 us -> 0 us
  Pallas kernels: 0 us -> 287 us
  blocking collectives: 75.8 us -> 0 us
  local copies, waits for them, and re-layouts: 60.5 us -> 13.1 us
  starting transfers between devices: 35.1 us -> 0 us
  matrix products: 27.6 us -> 0 us
    all_to_all x4 -> x0, waiting for transfers between devices: 557 us -> none  [the longest x1 276 us: on_device(): lax.all_to_all(slot_sums, 'shard', split_axis=0, concat_axis=0, tiled=True)]
    pallas_call x0 -> x1, Pallas kernels: none -> 287 us  [on_device(): pl.pallas_call(functools.partial(kernel, ny, nz, nx, total_points), out_s...]
    psum x1 -> x0, blocking collectives: 75.8 us -> none  [on_device(): spread = lax.psum(gap_total, ('shard', 'sub')) / total_points + 1e-06]
    all_to_all x4 -> x0, starting transfers between devices: 35.1 us -> none  [the longest x1 13.2 us: on_device(): lax.all_to_all(wanted, 'shard', split_axis=0, concat_axis=0, tiled=True)]
    dot_general x7 -> x0, matrix products: 27.6 us -> none  [the longest x1 15.5 us: on_device(): jnp.dot(slot_table, part, preferred_element_type=jnp.float32, precision=l...]
    dot_general x1 -> x0, local copies, waits for them, and re-layouts: 22.8 us -> none  [on_device(): jnp.dot(pick_table, half, preferred_element_type=jnp.bfloat16)]
    unnamed x15 -> x2, local copies, waits for them, and re-layouts: 20.8 us -> 1.08 us
  transfers between devices with their start and end apart: 4 -> 0, of which waited for: 3 -> 0; matrix products, arithmetic and copies ran while one was open for 3% -> 0% of each run, Pallas kernels for 0% -> 0%
where the time goes in v1:
time: 312 us
  Pallas kernels  287 us (92%)
  local copies, waits for them, and re-layouts  13.1 us (4%)
  other arithmetic  12.1 us (4%)
    pallas_call x1, Pallas kernels, on_device(): pl.pallas_call(functools.partial(kernel, ny, nz, nx, total_points), out_s...  287 us

profile of v1, /device:TPU:1, one launch (start us, length us, event | category | flops | bytes accessed | tf_op | source)
XLA Modules:
  0.0 311.8 jit_solution(11367004705958455857)
XLA Ops:
  0.0 0.8 eq.22
  0.8 0.2 fusion.1
  1.0 0.8 compare_reduce_fusion
  1.7 0.8 reshape.63
  2.5 2.4 multiply_reduce_fusion
  4.9 0.1 copy.11
  5.0 0.7 broadcast_in_dim.22.req_ref
  5.6 0.1 broadcast_in_dim.23
  5.7 0.6 copy.15
  6.3 2.0 convert_element_type.21
  8.4 0.4 reshape.61
  8.8 2.2 copy.10
  10.9 286.5 %shard_map.46 = (bf16[3,16,8,16,128]{4,3,2,1,0:T(8,128)(2,1)}, f32[16,16,128]{2,1,0:T(8,128)}) custom-call(bf16[1024,768]{1,0:T(8,128)(2,1)} %x_ref.1, bf16[3,16,8,16,128]{4,3,2,1,0:T(8,128)(2,1)} %bitcast.17, f32[1,1024]{1,0:T(1,128)} %bitcast.22, s32[16,128]{1,0:T(8,128)} %broadcast_in_dim.22.req_ref, f32[16,1024]{1,0:T(8,128)} %bitcast.19), custom_call_target="tpu_custom_call" | custom-call | tf_op jit(solution)/shard_map/pallas_call | solution.py:367
  297.5 0.8 slice.4
  298.3 0.4 copy.14
  298.8 0.2 add.35
  298.9 1.8 convert_bitcast_fusion
  300.8 2.4 copy.12
  303.2 3.7 %reshape.66 = f32[1024,768]{1,0:T(8,128)} reshape(f32[8,8,8,2,3,2,128]{6,5,4,3,2,1,0:T(2,128)S(1)} %copy.12) | data formatting | bytes 6291456 | tf_op jit(solution)/shard_map/convert_element_type | solution.py:408
  306.9 4.9 %add_divide_fusion = f32[1024,768]{1,0:T(8,128)} fusion(f32[1024,768]{1,0:T(8,128)} %reshape.66, f32[1024,768]{1,0:T(8,128)} %param.5, f32[1024]{0:T(1024)S(1)} %add.35), kind=kLoop, calls=%fused_computation.1 | loop fusion | flops 1572864 | bytes 9441280 | tf_op jit(solution)/shard_map/div | solution.py:411
  (4 shorter events, 0.0 us)

commit v2 on v0

v2 whole, which is shorter than its diff:
```python
import functools

import jax
import jax.numpy as jnp
from jax import lax
from jax.experimental import pallas as pl
from jax.experimental.pallas import tpu as pltpu
from jax.sharding import PartitionSpec as P

PBLK = 256
CBLK = 128
CAND = 4
NBLK = 4
OWNED = 8
PAIRS = CBLK // 2
ROWS = 2 * OWNED
SLOTS = 2 * NBLK * CAND
NQ = 3
WIDE = 256
LANES = 128
VMEM_LIMIT = 56 * 1024 * 1024
MESH = pl.DeviceIdType.MESH
F32 = jnp.float32
BF16 = jnp.bfloat16


def wait_bytes(ref, sem):
    pltpu.make_async_copy(ref, ref, sem).wait()


def iota(shape, dim):
    return lax.broadcasted_iota(jnp.int32, shape, dim)


def kernel(
    n,
    nx,
    total_points,
    x_ref,
    c_ref,
    req_ref,
    out_ref,
    rq,
    onehot,
    onehot_t,
    deal,
    held,
    pick,
    got,
    csq,
    dist,
    resp,
    part,
    back,
    final,
    home,
    w_part,
    w_back,
    w_final,
    w_home,
    gap_own,
    gap_all,
    gap_x,
    send_sem,
    recv_sem,
):
    rp = PAIRS // n
    keys = n * ROWS
    me = lax.axis_index("shard")
    sub = lax.axis_index("sub")

    barrier = pltpu.get_barrier_semaphore()

    def greet(off, carry):
        pl.semaphore_signal(
            barrier, inc=1, device_id=(lax.rem(me + off, n), sub), device_id_type=MESH
        )
        return carry

    lax.fori_loop(1, n, greet, 0)
    for off in range(1, nx):
        pl.semaphore_signal(
            barrier, inc=1, device_id=(me, lax.rem(sub + off, nx)), device_id_type=MESH
        )

    out_row = iota((LANES, LANES), 0)
    in_row = iota((LANES, LANES), 1)
    to_rows = jnp.where(in_row == lax.rem(out_row, ROWS) * OWNED + lax.div(out_row, ROWS), 1.0, 0.0)
    to_pairs = jnp.where(
        out_row == lax.rem(in_row, ROWS) * OWNED + lax.div(in_row, ROWS), 1.0, 0.0
    ).astype(BF16)
    for g in range(PAIRS // 8):
        half = c_ref[:, g * 16 : (g + 1) * 16].astype(BF16).reshape(LANES, NQ * WIDE)
        deal[g * 8 : (g + 1) * 8] = (
            jnp.dot(to_pairs, half, preferred_element_type=F32)
            .astype(BF16)
            .reshape(8, ROWS, NQ * WIDE)
        )

    pl.semaphore_wait(barrier, n - 1 + nx - 1)

    def send(src_of, dst_of, sem):
        def body(off, carry):
            k = lax.rem(me + off, n)
            pltpu.make_async_remote_copy(
                src_ref=src_of(k),
                dst_ref=dst_of(me),
                send_sem=send_sem.at[sem],
                recv_sem=recv_sem.at[sem],
                device_id=(k, sub),
                device_id_type=MESH,
            ).start()
            return carry

        lax.fori_loop(1, n, body, 0)
        pltpu.make_async_copy(src_of(me), dst_of(me), recv_sem.at[sem]).start()

    REQ, GAP, GAP_X, W4, W6, S1 = range(6)
    S3, S4, S6 = (6 + NQ * s for s in range(3))

    def mine(k):
        return pl.ds(k * rp, rp)

    send(lambda k: req_ref, lambda k: rq.at[k], REQ)
    send(lambda k: deal.at[mine(k)], lambda k: held.at[k], S1)

    wait_bytes(rq, recv_sem.at[REQ])

    def build(d, carry):
        here = iota((SLOTS, LANES), 1) == lax.rem(d, 4) * SLOTS + iota((SLOTS, LANES), 0)
        code = jnp.sum(jnp.where(here, rq[d], 0.0), axis=1, keepdims=True)
        for t in range(keys // LANES):
            lane = (iota((SLOTS, LANES), 1) + t * LANES).astype(F32)
            onehot[d, :, t * LANES : (t + 1) * LANES] = jnp.where(code == lane, 1.0, 0.0).astype(BF16)
        return carry

    lax.fori_loop(0, n, build, 0)
    key = iota((keys, LANES), 0).astype(F32)
    for t in range(n // 4):
        code = rq[4 * t] + rq[4 * t + 1] + rq[4 * t + 2] + rq[4 * t + 3]
        onehot_t[:, t * LANES : (t + 1) * LANES] = jnp.where(key == code, 1.0, 0.0).astype(BF16)
    square = jnp.zeros((x_ref.shape[0], LANES), F32)
    for t in range(NQ * WIDE // LANES):
        square = square + jnp.square(x_ref[:, t * LANES : (t + 1) * LANES].astype(F32))
    xsq = lax.dot_general(
        jnp.ones((8, LANES), F32),
        square,
        (((1,), (1,)), ((), ())),
        preferred_element_type=F32,
        precision=lax.Precision.HIGHEST,
    )[:1]

    wait_bytes(held, recv_sem.at[S1])
    some = 8
    for q in range(NQ):
        cols = slice(q * WIDE, (q + 1) * WIDE)

        def select(b, carry):
            here = pl.ds(b * some, some)
            table = onehot[here].reshape(some * SLOTS, keys)
            for r in range(rp):
                chosen = jnp.dot(
                    table, held[:, r, :, cols].reshape(keys, WIDE), preferred_element_type=F32
                )
                pick[q, here, r] = chosen.astype(BF16).reshape(some, SLOTS, WIDE)
            return carry

        lax.fori_loop(0, n // some, select, 0)
        send(lambda k: pick.at[q, k], lambda k: got.at[q, mine(k)], S3 + q)

    step = 16
    stats = []
    for q in range(NQ):
        cols = slice(q * WIDE, (q + 1) * WIDE)
        wait_bytes(got.at[q], recv_sem.at[S3 + q])
        for t in range(NBLK // 2):
            pts = slice(t * 2 * PBLK, (t + 1) * 2 * PBLK)

            def multiply(b, carry):
                here = pl.ds(b * step, step)
                rows = got[q, here, t * 16 : (t + 1) * 16].reshape(step * 16, WIDE)
                dots = lax.dot_general(
                    rows, x_ref[pts, cols], (((1,), (1,)), ((), ())), preferred_element_type=F32
                ).reshape(step, 2, 8, 2 * PBLK)
                wide = jnp.square(rows.astype(F32))
                sq = (wide[:, :LANES] + wide[:, LANES:]).reshape(step, 2, 8, LANES)
                after = []
                for i2 in range(2):
                    i = 2 * t + i2
                    dot = dots[:, i2, :, i2 * PBLK : (i2 + 1) * PBLK]
                    s = sq[:, i2]
                    if q > 0:
                        dot = dist[i, here] + dot
                        s = csq[i, here] + s
                    if q < NQ - 1:
                        dist[i, here] = dot
                        csq[i, here] = s
                    else:
                        x2 = xsq[:, i * PBLK : (i + 1) * PBLK]
                        d = (x2[None] + jnp.sum(s, axis=2, keepdims=True)) - 2.0 * dot
                        dist[i, here] = d
                        after.append(jnp.minimum(carry[2 * i2], jnp.min(d, axis=0)))
                        after.append(carry[2 * i2 + 1] + jnp.sum(d, axis=0))
                return tuple(after)

            start = ()
            if q == NQ - 1:
                start = (jnp.full((8, PBLK), jnp.inf, F32), jnp.zeros((8, PBLK), F32)) * 2
            found = lax.fori_loop(0, PAIRS // step, multiply, start)
            if q == NQ - 1:
                stats += [found[:2], found[2:]]
    least = [jnp.min(m, axis=0, keepdims=True) for m, _ in stats]
    gap = jnp.zeros((1, PBLK), F32)
    for i in range(NBLK):
        gap = gap + (jnp.sum(stats[i][1], axis=0, keepdims=True) / (CAND * CBLK) - least[i])

    gap_own[0] = jnp.broadcast_to(jnp.sum(gap, axis=1, keepdims=True), (1, LANES))
    send(lambda k: gap_own.at[0], lambda k: gap_all.at[k], GAP)
    wait_bytes(gap_all, recv_sem.at[GAP])
    gap_own[1] = jnp.sum(gap_all[...], axis=0)
    gap_x[sub] = gap_own[1]
    for off in range(1, nx):
        pltpu.make_async_remote_copy(
            src_ref=gap_own.at[1],
            dst_ref=gap_x.at[sub],
            send_sem=send_sem.at[GAP_X],
            recv_sem=recv_sem.at[GAP_X],
            device_id=(me, lax.rem(sub + off, nx)),
            device_id_type=MESH,
        ).start()
    if nx > 1:
        wait_bytes(gap_x.at[pl.ds(0, nx - 1)], recv_sem.at[GAP_X])
    spread = jnp.sum(gap_x[...], axis=0)[:, :1] / total_points + 1e-6
    scale = 3.0 / spread

    for i in range(NBLK):

        def exponent(b, norm):
            here = pl.ds(b * step, step)
            e = jnp.exp((least[i][None] - dist[i, here]) * scale[None])
            dist[i, here] = e
            return norm + jnp.sum(e, axis=0)

        norm = lax.fori_loop(0, PAIRS // step, exponent, jnp.zeros((8, PBLK), F32))
        inverse = 1.0 / jnp.sum(norm, axis=0, keepdims=True)

        def normalise(b, carry):
            e = dist[i, pl.ds(b * step, step)]
            resp[i, pl.ds(b * step * 8, step * 8)] = (
                (e * inverse[None]).reshape(step * 8, PBLK).astype(BF16)
            )
            return carry

        lax.fori_loop(0, PAIRS // step, normalise, 0)

    for q in range(NQ):
        cols = slice(q * WIDE, (q + 1) * WIDE)

        def accumulate(b, carry):
            here = pl.ds(b * step * 8, step * 8)
            for t in range(NBLK // 2):
                two = [
                    jnp.dot(
                        resp[i, here],
                        x_ref[i * PBLK : (i + 1) * PBLK, cols],
                        preferred_element_type=F32,
                    ).reshape(step, 8, WIDE)
                    for i in (2 * t, 2 * t + 1)
                ]
                part[q, pl.ds(b * step, step), t * 16 : (t + 1) * 16] = jnp.concatenate(
                    two, axis=1
                ).astype(BF16)
            return carry

        lax.fori_loop(0, PAIRS // step, accumulate, 0)
        send(lambda k: part.at[q, mine(k)], lambda k: back.at[q, k], S4 + q)
    for i in range(NBLK):
        mass = lax.dot_general(
            jnp.ones((8, PBLK), BF16), resp[i], (((1,), (1,)), ((), ())), preferred_element_type=F32
        )[:1]
        mass = mass.astype(BF16).astype(F32)
        for t in range(CAND):
            w_part[t, i] = mass[:, t * LANES : (t + 1) * LANES]
    per_tile = LANES // (8 * rp)
    send(lambda k: w_part.at[lax.div(k, per_tile)], lambda k: w_back.at[k], W4)

    for q in range(NQ):
        wait_bytes(back.at[q], recv_sem.at[S4 + q])

        def combine(b, carry):
            table = onehot_t[pl.ds(b * some * ROWS, some * ROWS)]
            for r in range(rp):
                added = jnp.dot(
                    table, back[q, :, r].reshape(n * SLOTS, WIDE), preferred_element_type=F32
                )
                final[q, pl.ds(b * some, some), r] = added.astype(BF16).reshape(some, ROWS, WIDE)
            return carry

        lax.fori_loop(0, n // some, combine, 0)
        send(lambda k: final.at[q, k], lambda k: home.at[q, mine(k)], S6 + q)
    wait_bytes(w_back, recv_sem.at[W4])
    first = lax.rem(me, per_tile) * 8 * rp
    lane = iota((n, ROWS, LANES), 2)
    row = iota((n, ROWS, LANES), 1)
    weight = jnp.zeros((n, 1, LANES), F32)
    for r in range(rp):
        spot = iota((n, NBLK, 8, LANES), 3) == iota((n, NBLK, 8, LANES), 2) + first + 8 * r
        wide = jnp.where(spot, w_back[...], 0.0).reshape(n * SLOTS, LANES).astype(BF16)
        added = jnp.dot(onehot_t[...], wide, preferred_element_type=F32)
        added = jnp.sum(added, axis=1, keepdims=True).reshape(n, ROWS, 1)
        weight = weight + jnp.sum(
            jnp.where(lane == row + ROWS * r, added, 0.0), axis=1, keepdims=True
        )
    w_final[...] = weight
    send(lambda k: w_final.at[k], lambda k: w_home.at[k], W6)

    wait_bytes(w_home, recv_sem.at[W6])
    for q in range(NQ):
        wait_bytes(home.at[q], recv_sem.at[S6 + q])
    spot = iota((8, ROWS, LANES), 2) == iota((8, ROWS, LANES), 1) + ROWS * lax.rem(
        iota((8, ROWS, LANES), 0), rp
    )
    own = 8 // rp
    for g in range(PAIRS // 8):
        wide = jnp.broadcast_to(w_home[g * own : (g + 1) * own][:, None], (own, rp, 1, LANES))
        wide = jnp.where(spot, wide.reshape(8, 1, LANES), 0.0).reshape(LANES, LANES)
        wide = jnp.dot(
            to_rows, wide, preferred_element_type=F32, precision=lax.Precision.HIGHEST
        )
        inverse = (1.0 / (jnp.sum(wide, axis=1, keepdims=True) + 1.0)).reshape(OWNED, 16, 1)
        for q in range(NQ):
            cols = slice(q * WIDE, (q + 1) * WIDE)
            sums = jnp.dot(
                to_rows.astype(BF16),
                home[q, g * 8 : (g + 1) * 8].reshape(LANES, WIDE),
                preferred_element_type=F32,
            ).reshape(OWNED, 16, WIDE)
            rows = slice(g * 16, (g + 1) * 16)
            out_ref[:, rows, cols] = (sums + 1.0 * c_ref[:, rows, cols]) * inverse

    others = pl.ds(0, n - 1)
    wait_bytes(rq.at[others], send_sem.at[REQ])
    wait_bytes(gap_all.at[others], send_sem.at[GAP])
    if nx > 1:
        wait_bytes(gap_x.at[pl.ds(0, nx - 1)], send_sem.at[GAP_X])
    wait_bytes(w_back.at[others], send_sem.at[W4])
    wait_bytes(w_final.at[others], send_sem.at[W6])
    wait_bytes(held.at[others], send_sem.at[S1])
    for q in range(NQ):
        wait_bytes(pick.at[q, others], send_sem.at[S3 + q])
        wait_bytes(back.at[q, others], send_sem.at[S4 + q])
        wait_bytes(final.at[q, others], send_sem.at[S6 + q])


def on_device(n, nx, points, centroids, cand_peer, cand_block):
    rp = PAIRS // n
    pts, width = points.shape
    code = cand_peer * ROWS + cand_block
    code = code[:, None, :] + OWNED * jnp.arange(2, dtype=jnp.int32)[None, :, None]
    code = jnp.tile(code.reshape(1, SLOTS), (1, LANES // SLOTS))
    place = jnp.arange(LANES, dtype=jnp.int32)[None, :] // SLOTS
    req = jnp.where(place == lax.axis_index("shard") % 4, code, 0).astype(F32)

    vmem = pl.BlockSpec(memory_space=pltpu.VMEM)
    n_sem = 6 + 3 * NQ
    refined = pl.pallas_call(
        functools.partial(kernel, n, nx, pts * n * nx),
        out_shape=jax.ShapeDtypeStruct((OWNED, CBLK, width), F32),
        in_specs=[vmem] * 3,
        out_specs=vmem,
        scratch_shapes=[
            pltpu.VMEM((n, 1, LANES), F32),
            pltpu.VMEM((n, SLOTS, n * ROWS), BF16),
            pltpu.VMEM((n * ROWS, n * SLOTS), BF16),
            pltpu.VMEM((PAIRS, ROWS, width), BF16),
            pltpu.VMEM((n, rp, ROWS, width), BF16),
            pltpu.VMEM((NQ, n, rp, SLOTS, WIDE), BF16),
            pltpu.VMEM((NQ, PAIRS, SLOTS, WIDE), BF16),
            pltpu.VMEM((NBLK, PAIRS, 8, LANES), F32),
            pltpu.VMEM((NBLK, PAIRS, 8, PBLK), F32),
            pltpu.VMEM((NBLK, PAIRS * 8, PBLK), BF16),
            pltpu.VMEM((NQ, PAIRS, SLOTS, WIDE), BF16),
            pltpu.VMEM((NQ, n, rp, SLOTS, WIDE), BF16),
            pltpu.VMEM((NQ, n, rp, ROWS, WIDE), BF16),
            pltpu.VMEM((NQ, PAIRS, ROWS, WIDE), BF16),
            pltpu.VMEM((CAND, NBLK, 1, LANES), F32),
            pltpu.VMEM((n, NBLK, 1, LANES), F32),
            pltpu.VMEM((n, 1, LANES), F32),
            pltpu.VMEM((n, 1, LANES), F32),
            pltpu.VMEM((2, 1, LANES), F32),
            pltpu.VMEM((n, 1, LANES), F32),
            pltpu.VMEM((nx, 1, LANES), F32),
            pltpu.SemaphoreType.DMA((n_sem,)),
            pltpu.SemaphoreType.DMA((n_sem,)),
        ],
        compiler_params=pltpu.CompilerParams(
            collective_id=0, has_side_effects=True, vmem_limit_bytes=VMEM_LIMIT
        ),
    )(points, centroids.reshape(OWNED, CBLK, width), req)
    return refined.reshape(OWNED * CBLK, width)


def solution(mesh):
    placed = P(("shard", "sub"), None)
    body = functools.partial(on_device, mesh.shape["shard"], mesh.shape["sub"])
    return jax.shard_map(
        body, mesh=mesh, in_specs=(placed,) * 4, out_specs=placed, check_vma=False
    )
```

time: 770 us -> 259 us (0.34)
  waiting for transfers between devices: 557 us -> 0 us
  Pallas kernels: 0 us -> 253 us
  blocking collectives: 75.8 us -> 0 us
  local copies, waits for them, and re-layouts: 60.5 us -> 3.93 us
  starting transfers between devices: 35.1 us -> 0 us
  matrix products: 27.6 us -> 0 us
  other arithmetic: 12.2 us -> 1.3 us
    all_to_all x4 -> x0, waiting for transfers between devices: 557 us -> none  [the longest x1 276 us: on_device(): lax.all_to_all(slot_sums, 'shard', split_axis=0, concat_axis=0, tiled=True)]
    pallas_call x0 -> x1, Pallas kernels: none -> 253 us  [on_device(): pl.pallas_call(functools.partial(kernel, n, nx, pts * n * nx), out_shape=...]
    psum x1 -> x0, blocking collectives: 75.8 us -> none  [on_device(): spread = lax.psum(gap_total, ('shard', 'sub')) / total_points + 1e-06]
    all_to_all x4 -> x0, starting transfers between devices: 35.1 us -> none  [the longest x1 13.2 us: on_device(): lax.all_to_all(wanted, 'shard', split_axis=0, concat_axis=0, tiled=True)]
    dot_general x7 -> x0, matrix products: 27.6 us -> none  [the longest x1 15.5 us: on_device(): jnp.dot(slot_table, part, preferred_element_type=jnp.float32, precision=l...]
    dot_general x1 -> x0, local copies, waits for them, and re-layouts: 22.8 us -> none  [on_device(): jnp.dot(pick_table, half, preferred_element_type=jnp.bfloat16)]
    unnamed x15 -> x1, local copies, waits for them, and re-layouts: 20.8 us -> 3.76 us
    reshape x4 -> x0, local copies, waits for them, and re-layouts: 10 us -> none  [the longest x1 5.11 us: on_device(): part = part.reshape(blocks_here * CAND, CBLK * width)]
  transfers between devices with their start and end apart: 4 -> 0, of which waited for: 3 -> 0; matrix products, arithmetic and copies ran while one was open for 3% -> 0% of each run, Pallas kernels for 0% -> 0%
where the time goes in v2:
time: 259 us; the launch traced here: 258 us
  Pallas kernels  253 us (98%)
  local copies, waits for them, and re-layouts  3.93 us (2%)
    pallas_call x1, Pallas kernels, on_device(): pl.pallas_call(functools.partial(kernel, n, nx, pts * n * nx), out_shape=...  253 us

profile of v2, /device:TPU:1, one launch (start us, length us, event | category | flops | bytes accessed | tf_op | source)
XLA Modules:
  0.0 258.4 jit_solution(9688673419951794774)
XLA Ops:
  0.0 0.7 multiply_add_fusion
  0.7 0.1 broadcast_add_fusion
  0.8 0.1 add.41
  0.9 0.1 tile.9
  1.0 0.5 fusion.req_ref
  1.5 253.2 %shard_map.46 = f32[8,128,768]{2,1,0:T(8,128)} custom-call(bf16[1024,768]{1,0:T(8,128)(2,1)} %x_ref.1, f32[8,128,768]{2,1,0:T(8,128)} %bitcast.3, f32[1,128]{1,0:T(1,128)} %fusion.req_ref), custom_call_target="tpu_custom_call" | custom-call | tf_op jit(solution)/shard_map/pallas_call | solution.py:366
  254.7 3.8 %copy.6 = f32[1024,768]{1,0:T(8,128)} copy(f32[1024,768]{1,0:T(8,128)} %bitcast.2) | data formatting | bytes 6291456
  (2 shorter events, 0.0 us)

commit v3 on v2

--- a/solution.py
+++ b/solution.py
@@ -36,10 +36,12 @@
     n,
     nx,
     total_points,
+    x_hbm,
+    c_hbm,
+    req_ref,
+    out_ref,
     x_ref,
     c_ref,
-    req_ref,
-    out_ref,
     rq,
     onehot,
     onehot_t,
@@ -59,15 +61,24 @@
     w_final,
     w_home,
     gap_own,
-    gap_all,
+    gap_lo,
+    gap_hi,
     gap_x,
     send_sem,
     recv_sem,
+    load_sem,
 ):
     rp = PAIRS // n
     keys = n * ROWS
+    low = gap_lo.shape[0]
+    high = n // low
     me = lax.axis_index("shard")
     sub = lax.axis_index("sub")
+
+    load_c = pltpu.make_async_copy(c_hbm, c_ref, load_sem.at[0])
+    load_x = pltpu.make_async_copy(x_hbm, x_ref, load_sem.at[1])
+    load_c.start()
+    load_x.start()
 
     barrier = pltpu.get_barrier_semaphore()
 
@@ -77,7 +88,7 @@
         )
         return carry
 
-    lax.fori_loop(1, n, greet, 0)
+    lax.fori_loop(1, n, greet, 0, unroll=7)
     for off in range(1, nx):
         pl.semaphore_signal(
             barrier, inc=1, device_id=(me, lax.rem(sub + off, nx)), device_id_type=MESH
@@ -89,14 +100,16 @@
     to_pairs = jnp.where(
         out_row == lax.rem(in_row, ROWS) * OWNED + lax.div(in_row, ROWS), 1.0, 0.0
     ).astype(BF16)
-    for g in range(PAIRS // 8):
-        half = c_ref[:, g * 16 : (g + 1) * 16].astype(BF16).reshape(LANES, NQ * WIDE)
-        deal[g * 8 : (g + 1) * 8] = (
-            jnp.dot(to_pairs, half, preferred_element_type=F32)
-            .astype(BF16)
-            .reshape(8, ROWS, NQ * WIDE)
-        )
-
+    load_c.wait()
+
+    def fill(q):
+        for g in range(PAIRS // 8):
+            half = c_ref[:, g * 16 : (g + 1) * 16, q * WIDE : (q + 1) * WIDE]
+            half = half.astype(BF16).reshape(LANES, WIDE)
+            paired = jnp.dot(to_pairs, half, preferred_element_type=F32)
+            deal[q, g * 8 : (g + 1) * 8] = paired.astype(BF16).reshape(8, ROWS, WIDE)
+
+    fill(0)
     pl.semaphore_wait(barrier, n - 1 + nx - 1)
 
     def send(src_of, dst_of, sem):
@@ -112,17 +125,21 @@
             ).start()
             return carry
 
-        lax.fori_loop(1, n, body, 0)
+        lax.fori_loop(1, n, body, 0, unroll=7)
         pltpu.make_async_copy(src_of(me), dst_of(me), recv_sem.at[sem]).start()
 
-    REQ, GAP, GAP_X, W4, W6, S1 = range(6)
-    S3, S4, S6 = (6 + NQ * s for s in range(3))
+    REQ, GAP_LO, GAP_HI, GAP_X, W4, W6, S1, S1_REST = range(8)
+    S3, S4, S6 = (8 + NQ * s for s in range(3))
 
     def mine(k):
         return pl.ds(k * rp, rp)
 
+    rest = pl.ds(1, NQ - 1)
+    send(lambda k: deal.at[0, mine(k)], lambda k: held.at[0, k], S1)
     send(lambda k: req_ref, lambda k: rq.at[k], REQ)
-    send(lambda k: deal.at[mine(k)], lambda k: held.at[k], S1)
+    for q in range(1, NQ):
+        fill(q)
+    send(lambda k: deal.at[rest, mine(k)], lambda k: held.at[rest, k], S1_REST)
 
     wait_bytes(rq, recv_sem.at[REQ])
 
@@ -135,6 +152,27 @@
         return carry
 
     lax.fori_loop(0, n, build, 0)
+    some = 8
+    for q in range(NQ):
+        if q == 0:
+            wait_bytes(held.at[0], recv_sem.at[S1])
+        if q == 1:
+            wait_bytes(held.at[rest], recv_sem.at[S1_REST])
+
+        def select(b, carry):
+            here = pl.ds(b * some, some)
+            table = onehot[here].reshape(some * SLOTS, keys)
+            for r in range(rp):
+                chosen = jnp.dot(
+                    table, held[q, :, r].reshape(keys, WIDE), preferred_element_type=F32
+                )
+                pick[q, here, r] = chosen.astype(BF16).reshape(some, SLOTS, WIDE)
+            return carry
+
+        lax.fori_loop(0, n // some, select, 0)
+        send(lambda k: pick.at[q, k], lambda k: got.at[q, mine(k)], S3 + q)
+
+    load_x.wait()
     key = iota((keys, LANES), 0).astype(F32)
     for t in range(n // 4):
         code = rq[4 * t] + rq[4 * t + 1] + rq[4 * t + 2] + rq[4 * t + 3]
@@ -149,24 +187,6 @@
         preferred_element_type=F32,
         precision=lax.Precision.HIGHEST,
     )[:1]
-
-    wait_bytes(held, recv_sem.at[S1])
-    some = 8
-    for q in range(NQ):
-        cols = slice(q * WIDE, (q + 1) * WIDE)
-
-        def select(b, carry):
-            here = pl.ds(b * some, some)
-            table = onehot[here].reshape(some * SLOTS, keys)
-            for r in range(rp):
-                chosen = jnp.dot(
-                    table, held[:, r, :, cols].reshape(keys, WIDE), preferred_element_type=F32
-                )
-                pick[q, here, r] = chosen.astype(BF16).reshape(some, SLOTS, WIDE)
-            return carry
-
-        lax.fori_loop(0, n // some, select, 0)
-        send(lambda k: pick.at[q, k], lambda k: got.at[q, mine(k)], S3 + q)
 
     step = 16
     stats = []
@@ -215,22 +235,32 @@
         gap = gap + (jnp.sum(stats[i][1], axis=0, keepdims=True) / (CAND * CBLK) - least[i])
 
     gap_own[0] = jnp.broadcast_to(jnp.sum(gap, axis=1, keepdims=True), (1, LANES))
-    send(lambda k: gap_own.at[0], lambda k: gap_all.at[k], GAP)
-    wait_bytes(gap_all, recv_sem.at[GAP])
-    gap_own[1] = jnp.sum(gap_all[...], axis=0)
-    gap_x[sub] = gap_own[1]
-    for off in range(1, nx):
-        pltpu.make_async_remote_copy(
-            src_ref=gap_own.at[1],
-            dst_ref=gap_x.at[sub],
-            send_sem=send_sem.at[GAP_X],
-            recv_sem=recv_sem.at[GAP_X],
-            device_id=(me, lax.rem(sub + off, nx)),
-            device_id_type=MESH,
-        ).start()
-    if nx > 1:
-        wait_bytes(gap_x.at[pl.ds(0, nx - 1)], recv_sem.at[GAP_X])
-    spread = jnp.sum(gap_x[...], axis=0)[:, :1] / total_points + 1e-6
+    lo = lax.rem(me, low)
+    hi = lax.div(me, low)
+
+    def share(of, into, at, devices, sem):
+        into[at] = gap_own[of]
+        for device in devices:
+            pltpu.make_async_remote_copy(
+                src_ref=gap_own.at[of],
+                dst_ref=into.at[at],
+                send_sem=send_sem.at[sem],
+                recv_sem=recv_sem.at[sem],
+                device_id=device,
+                device_id_type=MESH,
+            ).start()
+        if devices:
+            wait_bytes(into.at[pl.ds(0, len(devices))], recv_sem.at[sem])
+        return jnp.sum(into[...], axis=0)
+
+    gap_own[1] = share(
+        0, gap_lo, lo, [(hi * low + lax.rem(lo + o, low), sub) for o in range(1, low)], GAP_LO
+    )
+    gap_own[2] = share(
+        1, gap_hi, hi, [(lax.rem(hi + o, high) * low + lo, sub) for o in range(1, high)], GAP_HI
+    )
+    every = share(2, gap_x, sub, [(me, lax.rem(sub + o, nx)) for o in range(1, nx)], GAP_X)
+    spread = every[:, :1] / total_points + 1e-6
     scale = 3.0 / spread
 
     for i in range(NBLK):
@@ -252,6 +282,8 @@
             return carry
 
         lax.fori_loop(0, PAIRS // step, normalise, 0)
+
+    per_tile = LANES // (8 * rp)
 
     for q in range(NQ):
         cols = slice(q * WIDE, (q + 1) * WIDE)
@@ -274,15 +306,15 @@
 
         lax.fori_loop(0, PAIRS // step, accumulate, 0)
         send(lambda k: part.at[q, mine(k)], lambda k: back.at[q, k], S4 + q)
-    for i in range(NBLK):
-        mass = lax.dot_general(
-            jnp.ones((8, PBLK), BF16), resp[i], (((1,), (1,)), ((), ())), preferred_element_type=F32
-        )[:1]
-        mass = mass.astype(BF16).astype(F32)
-        for t in range(CAND):
-            w_part[t, i] = mass[:, t * LANES : (t + 1) * LANES]
-    per_tile = LANES // (8 * rp)
-    send(lambda k: w_part.at[lax.div(k, per_tile)], lambda k: w_back.at[k], W4)
+        if q == 0:
+            for i in range(NBLK):
+                mass = lax.dot_general(
+                    jnp.ones((8, PBLK), BF16), resp[i], (((1,), (1,)), ((), ())), preferred_element_type=F32
+                )[:1]
+                mass = mass.astype(BF16).astype(F32)
+                for t in range(CAND):
+                    w_part[t, i] = mass[:, t * LANES : (t + 1) * LANES]
+            send(lambda k: w_part.at[lax.div(k, per_tile)], lambda k: w_back.at[k], W4)
 
     for q in range(NQ):
         wait_bytes(back.at[q], recv_sem.at[S4 + q])
@@ -298,54 +330,59 @@
 
         lax.fori_loop(0, n // some, combine, 0)
         send(lambda k: final.at[q, k], lambda k: home.at[q, mine(k)], S6 + q)
-    wait_bytes(w_back, recv_sem.at[W4])
-    first = lax.rem(me, per_tile) * 8 * rp
-    lane = iota((n, ROWS, LANES), 2)
-    row = iota((n, ROWS, LANES), 1)
-    weight = jnp.zeros((n, 1, LANES), F32)
-    for r in range(rp):
-        spot = iota((n, NBLK, 8, LANES), 3) == iota((n, NBLK, 8, LANES), 2) + first + 8 * r
-        wide = jnp.where(spot, w_back[...], 0.0).reshape(n * SLOTS, LANES).astype(BF16)
-        added = jnp.dot(onehot_t[...], wide, preferred_element_type=F32)
-        added = jnp.sum(added, axis=1, keepdims=True).reshape(n, ROWS, 1)
-        weight = weight + jnp.sum(
-            jnp.where(lane == row + ROWS * r, added, 0.0), axis=1, keepdims=True
-        )
-    w_final[...] = weight
-    send(lambda k: w_final.at[k], lambda k: w_home.at[k], W6)
+        if q == 0:
+            wait_bytes(w_back, recv_sem.at[W4])
+            first = lax.rem(me, per_tile) * 8 * rp
+            lane = iota((n, ROWS, LANES), 2)
+            row = iota((n, ROWS, LANES), 1)
+            weight = jnp.zeros((n, 1, LANES), F32)
+            for r in range(rp):
+                spot = iota((n, NBLK, 8, LANES), 3) == iota((n, NBLK, 8, LANES), 2) + first + 8 * r
+                wide = jnp.where(spot, w_back[...], 0.0).reshape(n * SLOTS, LANES).astype(BF16)
+                added = jnp.dot(onehot_t[...], wide, preferred_element_type=F32)
+                added = jnp.sum(added, axis=1, keepdims=True).reshape(n, ROWS, 1)
+                weight = weight + jnp.sum(
+                    jnp.where(lane == row + ROWS * r, added, 0.0), axis=1, keepdims=True
+                )
+            w_final[...] = weight
+            send(lambda k: w_final.at[k], lambda k: w_home.at[k], W6)
 
     wait_bytes(w_home, recv_sem.at[W6])
-    for q in range(NQ):
-        wait_bytes(home.at[q], recv_sem.at[S6 + q])
     spot = iota((8, ROWS, LANES), 2) == iota((8, ROWS, LANES), 1) + ROWS * lax.rem(
         iota((8, ROWS, LANES), 0), rp
     )
     own = 8 // rp
+    inverse = []
     for g in range(PAIRS // 8):
         wide = jnp.broadcast_to(w_home[g * own : (g + 1) * own][:, None], (own, rp, 1, LANES))
         wide = jnp.where(spot, wide.reshape(8, 1, LANES), 0.0).reshape(LANES, LANES)
         wide = jnp.dot(
             to_rows, wide, preferred_element_type=F32, precision=lax.Precision.HIGHEST
         )
-        inverse = (1.0 / (jnp.sum(wide, axis=1, keepdims=True) + 1.0)).reshape(OWNED, 16, 1)
-        for q in range(NQ):
-            cols = slice(q * WIDE, (q + 1) * WIDE)
+        wide = 1.0 / (jnp.sum(wide, axis=1, keepdims=True) + 1.0)
+        inverse.append(wide.reshape(OWNED, 16, 1))
+    for q in range(NQ):
+        cols = slice(q * WIDE, (q + 1) * WIDE)
+        wait_bytes(home.at[q], recv_sem.at[S6 + q])
+        for g in range(PAIRS // 8):
             sums = jnp.dot(
                 to_rows.astype(BF16),
                 home[q, g * 8 : (g + 1) * 8].reshape(LANES, WIDE),
                 preferred_element_type=F32,
             ).reshape(OWNED, 16, WIDE)
             rows = slice(g * 16, (g + 1) * 16)
-            out_ref[:, rows, cols] = (sums + 1.0 * c_ref[:, rows, cols]) * inverse
+            out_ref[:, rows, cols] = (sums + 1.0 * c_ref[:, rows, cols]) * inverse[g]
 
     others = pl.ds(0, n - 1)
     wait_bytes(rq.at[others], send_sem.at[REQ])
-    wait_bytes(gap_all.at[others], send_sem.at[GAP])
+    wait_bytes(gap_lo.at[pl.ds(0, low - 1)], send_sem.at[GAP_LO])
+    wait_bytes(gap_hi.at[pl.ds(0, high - 1)], send_sem.at[GAP_HI])
     if nx > 1:
         wait_bytes(gap_x.at[pl.ds(0, nx - 1)], send_sem.at[GAP_X])
     wait_bytes(w_back.at[others], send_sem.at[W4])
     wait_bytes(w_final.at[others], send_sem.at[W6])
-    wait_bytes(held.at[others], send_sem.at[S1])
+    wait_bytes(held.at[0, others], send_sem.at[S1])
+    wait_bytes(held.at[rest, others], send_sem.at[S1_REST])
     for q in range(NQ):
         wait_bytes(pick.at[q, others], send_sem.at[S3 + q])
         wait_bytes(back.at[q, others], send_sem.at[S4 + q])
@@ -362,18 +399,22 @@
     req = jnp.where(place == lax.axis_index("shard") % 4, code, 0).astype(F32)
 
     vmem = pl.BlockSpec(memory_space=pltpu.VMEM)
-    n_sem = 6 + 3 * NQ
+    n_sem = 8 + 3 * NQ
+    low = 8 if n >= 64 else 4
+    hbm = pl.BlockSpec(memory_space=pl.ANY)
     refined = pl.pallas_call(
         functools.partial(kernel, n, nx, pts * n * nx),
         out_shape=jax.ShapeDtypeStruct((OWNED, CBLK, width), F32),
-        in_specs=[vmem] * 3,
+        in_specs=[hbm, hbm, vmem],
         out_specs=vmem,
         scratch_shapes=[
+            pltpu.VMEM((pts, width), BF16),
+            pltpu.VMEM((OWNED, CBLK, width), F32),
             pltpu.VMEM((n, 1, LANES), F32),
             pltpu.VMEM((n, SLOTS, n * ROWS), BF16),
             pltpu.VMEM((n * ROWS, n * SLOTS), BF16),
-            pltpu.VMEM((PAIRS, ROWS, width), BF16),
-            pltpu.VMEM((n, rp, ROWS, width), BF16),
+            pltpu.VMEM((NQ, PAIRS, ROWS, WIDE), BF16),
+            pltpu.VMEM((NQ, n, rp, ROWS, WIDE), BF16),
             pltpu.VMEM((NQ, n, rp, SLOTS, WIDE), BF16),
             pltpu.VMEM((NQ, PAIRS, SLOTS, WIDE), BF16),
             pltpu.VMEM((NBLK, PAIRS, 8, LANES), F32),
@@ -387,11 +428,13 @@
             pltpu.VMEM((n, NBLK, 1, LANES), F32),
             pltpu.VMEM((n, 1, LANES), F32),
             pltpu.VMEM((n, 1, LANES), F32),
-            pltpu.VMEM((2, 1, LANES), F32),
-            pltpu.VMEM((n, 1, LANES), F32),
+            pltpu.VMEM((3, 1, LANES), F32),
+            pltpu.VMEM((low, 1, LANES), F32),
+            pltpu.VMEM((n // low, 1, LANES), F32),
             pltpu.VMEM((nx, 1, LANES), F32),
             pltpu.SemaphoreType.DMA((n_sem,)),
             pltpu.SemaphoreType.DMA((n_sem,)),
+            pltpu.SemaphoreType.DMA((2,)),
         ],
         compiler_params=pltpu.CompilerParams(
             collective_id=0, has_side_effects=True, vmem_limit_bytes=VMEM_LIMIT

time: 259 us -> 247 us (0.954)
  Pallas kernels: 253 us -> 242 us
    pallas_call x1, Pallas kernels: 253 us -> 242 us  [on_device(): pl.pallas_call(functools.partial(kernel, n, nx, pts * n * nx), out_shape=...]
where the time goes in v3:
time: 247 us
  Pallas kernels  242 us (98%)
  local copies, waits for them, and re-layouts  3.93 us (2%)
    pallas_call x1, Pallas kernels, on_device(): pl.pallas_call(functools.partial(kernel, n, nx, pts * n * nx), out_shape=...  242 us

profile of v3, /device:TPU:1, one launch (start us, length us, event | category | flops | bytes accessed | tf_op | source)
XLA Modules:
  0.0 247.1 jit_solution(7003623058389657870)
XLA Ops:
  0.0 0.7 multiply_add_fusion
  0.7 0.1 broadcast_add_fusion
  0.8 0.1 add.41
  0.9 0.1 tile.9
  1.0 0.5 fusion.req_ref
  1.5 241.9 %shard_map.46 = f32[8,128,768]{2,1,0:T(8,128)} custom-call(bf16[1024,768]{1,0:T(8,128)(2,1)} %x_hbm.1, f32[8,128,768]{2,1,0:T(8,128)} %bitcast.3, f32[1,128]{1,0:T(1,128)} %fusion.req_ref), custom_call_target="tpu_custom_call" | custom-call | tf_op jit(solution)/shard_map/pallas_call | solution.py:405
  243.4 3.8 %copy.6 = f32[1024,768]{1,0:T(8,128)} copy(f32[1024,768]{1,0:T(8,128)} %bitcast.2) | data formatting | bytes 6291456
  (2 shorter events, 0.0 us)

commit v4 on v3

--- a/solution.py
+++ b/solution.py
@@ -38,6 +38,9 @@
     total_points,
     x_hbm,
     c_hbm,
+    peer_ref,
+    block_ref,
+    out_hbm,
     req_ref,
     out_ref,
     x_ref,
@@ -63,10 +66,10 @@
     gap_own,
     gap_lo,
     gap_hi,
-    gap_x,
     send_sem,
     recv_sem,
     load_sem,
+    out_sem,
 ):
     rp = PAIRS // n
     keys = n * ROWS
@@ -74,6 +77,8 @@
     high = n // low
     me = lax.axis_index("shard")
     sub = lax.axis_index("sub")
+    lo = lax.rem(me, low)
+    hi = lax.div(me, low)
 
     load_c = pltpu.make_async_copy(c_hbm, c_ref, load_sem.at[0])
     load_x = pltpu.make_async_copy(x_hbm, x_ref, load_sem.at[1])
@@ -90,9 +95,9 @@
 
     lax.fori_loop(1, n, greet, 0, unroll=7)
     for off in range(1, nx):
-        pl.semaphore_signal(
-            barrier, inc=1, device_id=(me, lax.rem(sub + off, nx)), device_id_type=MESH
-        )
+        for up in range(high):
+            other = (lax.rem(hi + up, high) * low + lo, lax.rem(sub + off, nx))
+            pl.semaphore_signal(barrier, inc=1, device_id=other, device_id_type=MESH)
 
     out_row = iota((LANES, LANES), 0)
     in_row = iota((LANES, LANES), 1)
@@ -110,7 +115,17 @@
             deal[q, g * 8 : (g + 1) * 8] = paired.astype(BF16).reshape(8, ROWS, WIDE)
 
     fill(0)
-    pl.semaphore_wait(barrier, n - 1 + nx - 1)
+    lane = iota((1, LANES), 1)
+    code = jnp.zeros((1, LANES), jnp.int32)
+    for i in range(NBLK):
+        for j in range(CAND):
+            here = lax.rem(lane, SLOTS)
+            here = (lax.div(here, 2 * CAND) == i) & (lax.rem(here, CAND) == j)
+            code = jnp.where(here, peer_ref[i, j] * ROWS + block_ref[i, j], code)
+    code = code + OWNED * lax.rem(lax.div(lane, CAND), 2)
+    req_ref[...] = jnp.where(lax.div(lane, SLOTS) == lax.rem(me, 4), code, 0).astype(F32)
+
+    pl.semaphore_wait(barrier, n - 1 + (nx - 1) * high)
 
     def send(src_of, dst_of, sem):
         def body(off, carry):
@@ -128,8 +143,8 @@
         lax.fori_loop(1, n, body, 0, unroll=7)
         pltpu.make_async_copy(src_of(me), dst_of(me), recv_sem.at[sem]).start()
 
-    REQ, GAP_LO, GAP_HI, GAP_X, W4, W6, S1, S1_REST = range(8)
-    S3, S4, S6 = (8 + NQ * s for s in range(3))
+    REQ, GAP_LO, GAP_HI, W4, W6, S1, S1_REST = range(7)
+    S3, S4, S6 = (7 + NQ * s for s in range(3))
 
     def mine(k):
         return pl.ds(k * rp, rp)
@@ -235,8 +250,6 @@
         gap = gap + (jnp.sum(stats[i][1], axis=0, keepdims=True) / (CAND * CBLK) - least[i])
 
     gap_own[0] = jnp.broadcast_to(jnp.sum(gap, axis=1, keepdims=True), (1, LANES))
-    lo = lax.rem(me, low)
-    hi = lax.div(me, low)
 
     def share(of, into, at, devices, sem):
         into[at] = gap_own[of]
@@ -249,17 +262,18 @@
                 device_id=device,
                 device_id_type=MESH,
             ).start()
-        if devices:
+        if len(devices) > 0:
             wait_bytes(into.at[pl.ds(0, len(devices))], recv_sem.at[sem])
         return jnp.sum(into[...], axis=0)
 
     gap_own[1] = share(
         0, gap_lo, lo, [(hi * low + lax.rem(lo + o, low), sub) for o in range(1, low)], GAP_LO
     )
-    gap_own[2] = share(
-        1, gap_hi, hi, [(lax.rem(hi + o, high) * low + lo, sub) for o in range(1, high)], GAP_HI
-    )
-    every = share(2, gap_x, sub, [(me, lax.rem(sub + o, nx)) for o in range(1, nx)], GAP_X)
+    across = high * nx
+    place = hi * nx + sub
+    others = [lax.rem(place + o, across) for o in range(1, across)]
+    others = [(lax.div(o, nx) * low + lo, lax.rem(o, nx)) for o in others]
+    every = share(1, gap_hi, place, others, GAP_HI)
     spread = every[:, :1] / total_points + 1e-6
     scale = 3.0 / spread
 
@@ -372,13 +386,14 @@
             ).reshape(OWNED, 16, WIDE)
             rows = slice(g * 16, (g + 1) * 16)
             out_ref[:, rows, cols] = (sums + 1.0 * c_ref[:, rows, cols]) * inverse[g]
+        pltpu.make_async_copy(
+            out_ref.at[:, :, cols], out_hbm.at[:, :, cols], out_sem.at[q]
+        ).start()
 
     others = pl.ds(0, n - 1)
     wait_bytes(rq.at[others], send_sem.at[REQ])
     wait_bytes(gap_lo.at[pl.ds(0, low - 1)], send_sem.at[GAP_LO])
-    wait_bytes(gap_hi.at[pl.ds(0, high - 1)], send_sem.at[GAP_HI])
-    if nx > 1:
-        wait_bytes(gap_x.at[pl.ds(0, nx - 1)], send_sem.at[GAP_X])
+    wait_bytes(gap_hi.at[pl.ds(0, across - 1)], send_sem.at[GAP_HI])
     wait_bytes(w_back.at[others], send_sem.at[W4])
     wait_bytes(w_final.at[others], send_sem.at[W6])
     wait_bytes(held.at[0, others], send_sem.at[S1])
@@ -387,27 +402,28 @@
         wait_bytes(pick.at[q, others], send_sem.at[S3 + q])
         wait_bytes(back.at[q, others], send_sem.at[S4 + q])
         wait_bytes(final.at[q, others], send_sem.at[S6 + q])
+    for q in range(NQ):
+        cols = slice(q * WIDE, (q + 1) * WIDE)
+        pltpu.make_async_copy(
+            out_ref.at[:, :, cols], out_hbm.at[:, :, cols], out_sem.at[q]
+        ).wait()
 
 
 def on_device(n, nx, points, centroids, cand_peer, cand_block):
     rp = PAIRS // n
     pts, width = points.shape
-    code = cand_peer * ROWS + cand_block
-    code = code[:, None, :] + OWNED * jnp.arange(2, dtype=jnp.int32)[None, :, None]
-    code = jnp.tile(code.reshape(1, SLOTS), (1, LANES // SLOTS))
-    place = jnp.arange(LANES, dtype=jnp.int32)[None, :] // SLOTS
-    req = jnp.where(place == lax.axis_index("shard") % 4, code, 0).astype(F32)
-
-    vmem = pl.BlockSpec(memory_space=pltpu.VMEM)
-    n_sem = 8 + 3 * NQ
-    low = 8 if n >= 64 else 4
+    smem = pl.BlockSpec(memory_space=pltpu.SMEM)
+    n_sem = 7 + 3 * NQ
+    low = 16 if n >= 64 else 4
     hbm = pl.BlockSpec(memory_space=pl.ANY)
     refined = pl.pallas_call(
         functools.partial(kernel, n, nx, pts * n * nx),
         out_shape=jax.ShapeDtypeStruct((OWNED, CBLK, width), F32),
-        in_specs=[hbm, hbm, vmem],
-        out_specs=vmem,
+        in_specs=[hbm, hbm, smem, smem],
+        out_specs=hbm,
         scratch_shapes=[
+            pltpu.VMEM((1, LANES), F32),
+            pltpu.VMEM((OWNED, CBLK, width), F32),
             pltpu.VMEM((pts, width), BF16),
             pltpu.VMEM((OWNED, CBLK, width), F32),
             pltpu.VMEM((n, 1, LANES), F32),
@@ -428,18 +444,18 @@
             pltpu.VMEM((n, NBLK, 1, LANES), F32),
             pltpu.VMEM((n, 1, LANES), F32),
             pltpu.VMEM((n, 1, LANES), F32),
-            pltpu.VMEM((3, 1, LANES), F32),
+            pltpu.VMEM((2, 1, LANES), F32),
             pltpu.VMEM((low, 1, LANES), F32),
-            pltpu.VMEM((n // low, 1, LANES), F32),
-            pltpu.VMEM((nx, 1, LANES), F32),
+            pltpu.VMEM((n // low * nx, 1, LANES), F32),
             pltpu.SemaphoreType.DMA((n_sem,)),
             pltpu.SemaphoreType.DMA((n_sem,)),
             pltpu.SemaphoreType.DMA((2,)),
+            pltpu.SemaphoreType.DMA((NQ,)),
         ],
         compiler_params=pltpu.CompilerParams(
             collective_id=0, has_side_effects=True, vmem_limit_bytes=VMEM_LIMIT
         ),
-    )(points, centroids.reshape(OWNED, CBLK, width), req)
+    )(points, centroids.reshape(OWNED, CBLK, width), cand_peer, cand_block)
     return refined.reshape(OWNED * CBLK, width)
 
 

time: 247 us -> 243 us (0.984)
  Pallas kernels: 242 us -> 239 us
where the time goes in v4:
time: 243 us
  Pallas kernels  239 us (98%)
  local copies, waits for them, and re-layouts  3.76 us (2%)
    pallas_call x1, Pallas kernels, on_device(): pl.pallas_call(functools.partial(kernel, n, nx, pts * n * nx), out_shape=...  239 us

profile of v4, /device:TPU:1, one launch (start us, length us, event | category | flops | bytes accessed | tf_op | source)
XLA Modules:
  0.0 243.2 jit_solution(17933280989528595946)
XLA Ops:
  0.0 239.5 %shard_map.46 = f32[8,128,768]{2,1,0:T(8,128)} custom-call(bf16[1024,768]{1,0:T(8,128)(2,1)} %x_hbm.1, f32[8,128,768]{2,1,0:T(8,128)} %bitcast.3, s32[4,4]{1,0:T(4,128)} %peer_ref.1, s32[4,4]{1,0:T(4,128)} %block_ref.1), custom_call_target="tpu_custom_call" | custom-call | tf_op jit(solution)/shard_map/pallas_call | solution.py:419
  239.5 3.8 %copy.6 = f32[1024,768]{1,0:T(8,128)} copy(f32[1024,768]{1,0:T(8,128)} %bitcast.2) | data formatting | bytes 6291456

commit v5 on v4

--- a/solution.py
+++ b/solution.py
@@ -55,6 +55,7 @@
     csq,
     dist,
     resp,
+    pack,
     part,
     back,
     final,
@@ -188,6 +189,10 @@
         send(lambda k: pick.at[q, k], lambda k: got.at[q, mine(k)], S3 + q)
 
     load_x.wait()
+    src = iota((NBLK * LANES, NBLK * LANES), 0)
+    dst = lax.div(lax.rem(src, LANES), 32) * LANES + lax.div(lax.rem(src, 32), 8) * 32
+    dst = dst + lax.div(src, LANES) * 8 + lax.rem(src, 8)
+    pack[...] = jnp.where(iota((NBLK * LANES, NBLK * LANES), 1) == dst, 1.0, 0.0).astype(BF16)
     key = iota((keys, LANES), 0).astype(F32)
     for t in range(n // 4):
         code = rq[4 * t] + rq[4 * t + 1] + rq[4 * t + 2] + rq[4 * t + 3]
@@ -203,7 +208,7 @@
         precision=lax.Precision.HIGHEST,
     )[:1]
 
-    step = 16
+    step = 32
     stats = []
     for q in range(NQ):
         cols = slice(q * WIDE, (q + 1) * WIDE)
@@ -297,38 +302,50 @@
 
         lax.fori_loop(0, PAIRS // step, normalise, 0)
 
-    per_tile = LANES // (8 * rp)
+    tiles = max(1, rp // 4)
 
     for q in range(NQ):
         cols = slice(q * WIDE, (q + 1) * WIDE)
 
         def accumulate(b, carry):
-            here = pl.ds(b * step * 8, step * 8)
             for t in range(NBLK // 2):
                 two = [
                     jnp.dot(
-                        resp[i, here],
+                        resp[i],
                         x_ref[i * PBLK : (i + 1) * PBLK, cols],
                         preferred_element_type=F32,
-                    ).reshape(step, 8, WIDE)
+                    ).reshape(PAIRS, 8, WIDE)
                     for i in (2 * t, 2 * t + 1)
                 ]
-                part[q, pl.ds(b * step, step), t * 16 : (t + 1) * 16] = jnp.concatenate(
+                part[q, :, t * 16 : (t + 1) * 16] = jnp.concatenate(
                     two, axis=1
                 ).astype(BF16)
             return carry
 
-        lax.fori_loop(0, PAIRS // step, accumulate, 0)
+        accumulate(0, 0)
         send(lambda k: part.at[q, mine(k)], lambda k: back.at[q, k], S4 + q)
         if q == 0:
+            tile = iota((8, LANES), 0)
+            masses = []
             for i in range(NBLK):
                 mass = lax.dot_general(
-                    jnp.ones((8, PBLK), BF16), resp[i], (((1,), (1,)), ((), ())), preferred_element_type=F32
-                )[:1]
-                mass = mass.astype(BF16).astype(F32)
-                for t in range(CAND):
-                    w_part[t, i] = mass[:, t * LANES : (t + 1) * LANES]
-            send(lambda k: w_part.at[lax.div(k, per_tile)], lambda k: w_back.at[k], W4)
+                    jnp.ones((8, PBLK), BF16),
+                    resp[i],
+                    (((1,), (1,)), ((), ())),
+                    preferred_element_type=F32,
+                )
+                stacked = mass[:, :LANES]
+                for t in range(1, CAND):
+                    stacked = jnp.where(tile == t, mass[:, t * LANES : (t + 1) * LANES], stacked)
+                masses.append(stacked)
+            packed = jnp.concatenate(masses, axis=1).astype(BF16)
+            packed = jnp.dot(packed, pack[...], preferred_element_type=F32)
+            for t in range(CAND):
+                for v in range(NBLK):
+                    w_part[t * NBLK + v] = packed[t : t + 1, v * LANES : (v + 1) * LANES]
+            send(
+                lambda k: w_part.at[pl.ds(lax.div(k * rp, 4), tiles)], lambda k: w_back.at[k], W4
+            )
 
     for q in range(NQ):
         wait_bytes(back.at[q], recv_sem.at[S4 + q])
@@ -346,13 +363,14 @@
         send(lambda k: final.at[q, k], lambda k: home.at[q, mine(k)], S6 + q)
         if q == 0:
             wait_bytes(w_back, recv_sem.at[W4])
-            first = lax.rem(me, per_tile) * 8 * rp
             lane = iota((n, ROWS, LANES), 2)
             row = iota((n, ROWS, LANES), 1)
             weight = jnp.zeros((n, 1, LANES), F32)
             for r in range(rp):
-                spot = iota((n, NBLK, 8, LANES), 3) == iota((n, NBLK, 8, LANES), 2) + first + 8 * r
-                wide = jnp.where(spot, w_back[...], 0.0).reshape(n * SLOTS, LANES).astype(BF16)
+                first = lax.rem(me * rp + r, 4) * SLOTS
+                spot = iota((n, SLOTS, LANES), 2) == iota((n, SLOTS, LANES), 1) + first
+                wide = jnp.where(spot, w_back[:, r // 4], 0.0)
+                wide = wide.reshape(n * SLOTS, LANES).astype(BF16)
                 added = jnp.dot(onehot_t[...], wide, preferred_element_type=F32)
                 added = jnp.sum(added, axis=1, keepdims=True).reshape(n, ROWS, 1)
                 weight = weight + jnp.sum(
@@ -436,12 +454,13 @@
             pltpu.VMEM((NBLK, PAIRS, 8, LANES), F32),
             pltpu.VMEM((NBLK, PAIRS, 8, PBLK), F32),
             pltpu.VMEM((NBLK, PAIRS * 8, PBLK), BF16),
+            pltpu.VMEM((NBLK * LANES, NBLK * LANES), BF16),
             pltpu.VMEM((NQ, PAIRS, SLOTS, WIDE), BF16),
             pltpu.VMEM((NQ, n, rp, SLOTS, WIDE), BF16),
             pltpu.VMEM((NQ, n, rp, ROWS, WIDE), BF16),
             pltpu.VMEM((NQ, PAIRS, ROWS, WIDE), BF16),
-            pltpu.VMEM((CAND, NBLK, 1, LANES), F32),
-            pltpu.VMEM((n, NBLK, 1, LANES), F32),
+            pltpu.VMEM((PAIRS // 4, 1, LANES), F32),
+            pltpu.VMEM((n, max(1, rp // 4), 1, LANES), F32),
             pltpu.VMEM((n, 1, LANES), F32),
             pltpu.VMEM((n, 1, LANES), F32),
             pltpu.VMEM((2, 1, LANES), F32),

time: 243 us -> 240 us (0.988)
  Pallas kernels: 239 us -> 236 us
    pallas_call x1, Pallas kernels: 239 us -> 236 us  [on_device(): pl.pallas_call(functools.partial(kernel, n, nx, pts * n * nx), out_shape=...]
where the time goes in v5:
time: 240 us
  Pallas kernels  236 us (98%)
  local copies, waits for them, and re-layouts  3.76 us (2%)
    pallas_call x1, Pallas kernels, on_device(): pl.pallas_call(functools.partial(kernel, n, nx, pts * n * nx), out_shape=...  236 us

profile of v5, /device:TPU:1, one launch (start us, length us, event | category | flops | bytes accessed | tf_op | source)
XLA Modules:
  0.0 239.7 jit_solution(15813375709192464029)
XLA Ops:
  0.0 235.9 %shard_map.46 = f32[8,128,768]{2,1,0:T(8,128)} custom-call(bf16[1024,768]{1,0:T(8,128)(2,1)} %x_hbm.1, f32[8,128,768]{2,1,0:T(8,128)} %bitcast.3, s32[4,4]{1,0:T(4,128)} %peer_ref.1, s32[4,4]{1,0:T(4,128)} %block_ref.1), custom_call_target="tpu_custom_call" | custom-call | tf_op jit(solution)/shard_map/pallas_call | solution.py:437
  235.9 3.8 %copy.6 = f32[1024,768]{1,0:T(8,128)} copy(f32[1024,768]{1,0:T(8,128)} %bitcast.2) | data formatting | bytes 6291456

commit v6 on v5

--- a/solution.py
+++ b/solution.py
@@ -168,7 +168,8 @@
         return carry
 
     lax.fori_loop(0, n, build, 0)
-    some = 8
+    some = min(16, n)
+    many = min(32, n)
     for q in range(NQ):
         if q == 0:
             wait_bytes(held.at[0], recv_sem.at[S1])
@@ -208,7 +209,7 @@
         precision=lax.Precision.HIGHEST,
     )[:1]
 
-    step = 32
+    step = 64
     stats = []
     for q in range(NQ):
         cols = slice(q * WIDE, (q + 1) * WIDE)
@@ -351,15 +352,15 @@
         wait_bytes(back.at[q], recv_sem.at[S4 + q])
 
         def combine(b, carry):
-            table = onehot_t[pl.ds(b * some * ROWS, some * ROWS)]
+            table = onehot_t[pl.ds(b * many * ROWS, many * ROWS)]
             for r in range(rp):
                 added = jnp.dot(
                     table, back[q, :, r].reshape(n * SLOTS, WIDE), preferred_element_type=F32
                 )
-                final[q, pl.ds(b * some, some), r] = added.astype(BF16).reshape(some, ROWS, WIDE)
+                final[q, pl.ds(b * many, many), r] = added.astype(BF16).reshape(many, ROWS, WIDE)
             return carry
 
-        lax.fori_loop(0, n // some, combine, 0)
+        lax.fori_loop(0, n // many, combine, 0)
         send(lambda k: final.at[q, k], lambda k: home.at[q, mine(k)], S6 + q)
         if q == 0:
             wait_bytes(w_back, recv_sem.at[W4])

time: 240 us -> 239 us (level)
  no operation moved by 1% of the time
where the time goes in v6:
time: 239 us
  Pallas kernels  235 us (98%)
  local copies, waits for them, and re-layouts  3.76 us (2%)
    pallas_call x1, Pallas kernels, on_device(): pl.pallas_call(functools.partial(kernel, n, nx, pts * n * nx), out_shape=...  235 us

profile of v6, /device:TPU:1, one launch (start us, length us, event | category | flops | bytes accessed | tf_op | source)
XLA Modules:
  0.0 238.9 jit_solution(3904291931052803360)
XLA Ops:
  0.0 235.1 %shard_map.46 = f32[8,128,768]{2,1,0:T(8,128)} custom-call(bf16[1024,768]{1,0:T(8,128)(2,1)} %x_hbm.1, f32[8,128,768]{2,1,0:T(8,128)} %bitcast.3, s32[4,4]{1,0:T(4,128)} %peer_ref.1, s32[4,4]{1,0:T(4,128)} %block_ref.1), custom_call_target="tpu_custom_call" | custom-call | tf_op jit(solution)/shard_map/pallas_call | solution.py:438
  235.1 3.8 %copy.6 = f32[1024,768]{1,0:T(8,128)} copy(f32[1024,768]{1,0:T(8,128)} %bitcast.2) | data formatting | bytes 6291456

commit v7 on v6

--- a/solution.py
+++ b/solution.py
@@ -428,6 +428,19 @@
         ).wait()
 
 
+def hand_on(x_hbm, o_hbm, held, in_sem, out_sem):
+    rows = [pl.ds(b * CBLK, CBLK) for b in range(OWNED)]
+    into = [pltpu.make_async_copy(x_hbm.at[rows[b]], held.at[b], in_sem.at[b]) for b in range(OWNED)]
+    out = [pltpu.make_async_copy(held.at[b], o_hbm.at[rows[b]], out_sem.at[b]) for b in range(OWNED)]
+    for b in range(OWNED):
+        into[b].start()
+    for b in range(OWNED):
+        into[b].wait()
+        out[b].start()
+    for b in range(OWNED):
+        out[b].wait()
+
+
 def on_device(n, nx, points, centroids, cand_peer, cand_block):
     rp = PAIRS // n
     pts, width = points.shape
@@ -476,7 +489,17 @@
             collective_id=0, has_side_effects=True, vmem_limit_bytes=VMEM_LIMIT
         ),
     )(points, centroids.reshape(OWNED, CBLK, width), cand_peer, cand_block)
-    return refined.reshape(OWNED * CBLK, width)
+    return pl.pallas_call(
+        hand_on,
+        out_shape=jax.ShapeDtypeStruct((OWNED * CBLK, width), F32),
+        in_specs=[hbm],
+        out_specs=hbm,
+        scratch_shapes=[
+            pltpu.VMEM((OWNED, CBLK, width), F32),
+            pltpu.SemaphoreType.DMA((OWNED,)),
+            pltpu.SemaphoreType.DMA((OWNED,)),
+        ],
+    )(refined.reshape(OWNED * CBLK, width))
 
 
 def solution(mesh):

time: 239 us -> 238 us (level)
  local copies, waits for them, and re-layouts: 3.76 us -> 0 us
  Pallas kernels: 235 us -> 238 us
    unnamed x1 -> x0, local copies, waits for them, and re-layouts: 3.76 us -> none
    pallas_call x0 -> x1, Pallas kernels: none -> 2.79 us  [on_device(): pl.pallas_call(hand_on, out_shape=jax.ShapeDtypeStruct((OWNED * CBLK, wid...]
where the time goes in v7:
time: 238 us
  Pallas kernels  238 us (100%)
    pallas_call x1, Pallas kernels, on_device(): pl.pallas_call(functools.partial(kernel, n, nx, pts * n * nx), out_shape=...  235 us

profile of v7, /device:TPU:1, one launch (start us, length us, event | category | flops | bytes accessed | tf_op | source)
XLA Modules:
  0.0 237.9 jit_solution(795127705904975306)
XLA Ops:
  0.0 235.1 %shard_map.46 = f32[8,128,768]{2,1,0:T(8,128)} custom-call(bf16[1024,768]{1,0:T(8,128)(2,1)} %x_hbm.1, f32[8,128,768]{2,1,0:T(8,128)} %bitcast.3, s32[4,4]{1,0:T(4,128)} %peer_ref.1, s32[4,4]{1,0:T(4,128)} %block_ref.1), custom_call_target="tpu_custom_call" | custom-call | tf_op jit(solution)/shard_map/pallas_call | solution.py:451
  235.1 2.8 %shard_map.47 = f32[1024,768]{1,0:T(8,128)} custom-call(f32[1024,768]{1,0:T(8,128)} %bitcast.2), custom_call_target="tpu_custom_call" | custom-call | tf_op jit(solution)/shard_map/pallas_call | solution.py:492
